TPU v7x, 256 devices: a whole 4x4x8 slice. The times are simulated.
256 devices in a mesh: rows: 64 (over y_lo, z, x), rep: 4 (over y_hi, core).
Axes of the slice: x: 4, y: 4 (y_hi: 2, y_lo: 2; y = y_hi * 2 + y_lo), z: 8, core: 2. Of those that a mesh axis runs over, the one named last changes fastest.
Arguments:
- features: bfloat16 [131072, 128], P('rows'), may hold values from -6 to 6
- adjacency: bfloat16 [64, 4, 2, 40, 256, 256], P('rows', 'rep'), may hold values from -0.0625 to 0.0625
- tile_coords: int32 [64, 4, 2, 2, 40], P('rows', 'rep'), may hold values from 0 to 7, as said below
- tile_counts: int32 [64, 4, 2], P('rows', 'rep'), may hold values from 1 to 40, as said below
- weight: bfloat16 [128, 256], replicated, may hold values from -0.5 to 0.5
- bias: float32 [256], replicated, may hold values from -3 to 3
- cotangent: bfloat16 [131072, 256], P(('rows', 'rep'))
Outputs:
- hidden: bfloat16 [131072, 256], P(('rows', 'rep'))
- grad_inputs: bfloat16 [4, 2, 2048, 128], P('rep', None, 'rows')
- grad_weight: float32 [128, 256], replicated
- grad_bias: float32 [256], replicated
Inputs may be any that keep to these rules, and one draw needn't show every extreme that they name: tile_coords[i, g, s, 0, t] and tile_coords[i, g, s, 1, t] are the tile row in row block i and the tile column in column block c(g, s) of slot t; the 40 positions of one row block, group and section are distinct; slots at or past the count hold no tile. `tile_counts`: for every replica group and section some row block has exactly 40 live slots.
All inputs are finite; a program needn't handle non-finite values.
Results may differ from a plain program's by a relative error of at most 0.0059.
Values may be sent and summed in bfloat16 or wider, within the bound.
A program may use at most 128 MiB of HBM per device.

v0:
```python
import math

import jax
import jax.numpy as jnp
from jax import lax
from jax.sharding import PartitionSpec as P


def spread(value, axis, root):
    mine = lax.axis_index(axis) == root
    return lax.psum(jnp.where(mine, value, jnp.zeros_like(value)), axis)


def gelu_tanh(value):
    return jax.nn.gelu(value, approximate=True)


def pick_matrix(target, live_count, tiles_side):
    slot_count = target.shape[0]
    is_live = jnp.arange(slot_count, dtype=jnp.int32) < live_count
    same = jnp.arange(tiles_side, dtype=jnp.int32)[:, None] == target[None, :]
    return (same & is_live[None, :]).astype(jnp.float32)


def forward_tiles(tile_values, tile_place, live_count, column_tiles):
    chosen = column_tiles[tile_place[1]]
    products = jnp.einsum("tij,tjf->tif", tile_values, chosen, preferred_element_type=jnp.float32)
    placed = pick_matrix(tile_place[0], live_count, column_tiles.shape[0])
    return jnp.einsum("pt,tif->pif", placed, products, precision=lax.Precision.HIGHEST)


def backward_tiles(tile_values, tile_place, live_count, grad_tiles):
    chosen = grad_tiles[tile_place[0]]
    products = jnp.einsum("tji,tjf->tif", tile_values, chosen, preferred_element_type=jnp.float32)
    placed = pick_matrix(tile_place[1], live_count, grad_tiles.shape[0])
    return jnp.einsum("pt,tif->pif", placed, products, precision=lax.Precision.HIGHEST)


def shards(features, adjacency, tile_coords, tile_counts, weight, bias, cotangent):
    rows_count = lax.axis_size("rows")
    rep_count = lax.axis_size("rep")
    section_count = adjacency.shape[2]
    tile_size = adjacency.shape[4]
    block_rows = features.shape[0]
    feat_width = features.shape[1]
    tiles_side = block_rows // tile_size
    quarter = block_rows // rep_count
    spacing = rows_count // (rep_count * section_count)
    replica = lax.axis_index("rep")
    scale_factor = 1.0 / math.sqrt(block_rows * rows_count)
    partial_sum = jnp.zeros((tiles_side, tile_size, feat_width), jnp.float32)
    for section_index in range(section_count):
        owner_row = (replica * section_count + section_index) * spacing
        column_rows = spread(features, "rows", owner_row)
        partial_sum = partial_sum + forward_tiles(
            adjacency[0, 0, section_index],
            tile_coords[0, 0, section_index],
            tile_counts[0, 0, section_index],
            column_rows.reshape(tiles_side, tile_size, feat_width),
        )
    partial_sum = partial_sum.reshape(block_rows, feat_width)
    aggregate = lax.psum(partial_sum, "rep")
    aggregate_bf = aggregate.astype(jnp.bfloat16)
    preact = jnp.dot(aggregate_bf, weight, preferred_element_type=jnp.float32) + bias
    grad_out = lax.all_gather(cotangent, "rep", axis=0, tiled=True)
    activated, pullback = jax.vjp(gelu_tanh, preact)
    grad_pre = pullback(grad_out.astype(jnp.float32))[0]
    grad_pre_bf = grad_pre.astype(jnp.bfloat16)
    weight_term = lax.dot_general(
        aggregate_bf, grad_pre_bf, (((0,), (0,)), ((), ())), preferred_element_type=jnp.float32
    )
    bias_term = jnp.sum(grad_pre, axis=0)
    weight_total, bias_total = lax.psum((weight_term, bias_term), "rows")
    grad_rows = lax.dot_general(
        grad_pre_bf, weight, (((1,), (1,)), ((), ())), preferred_element_type=jnp.float32
    ).astype(jnp.bfloat16)
    hidden = lax.dynamic_slice_in_dim(activated, replica * quarter, quarter, 0).astype(jnp.bfloat16)
    grad_tiles = grad_rows.reshape(tiles_side, tile_size, feat_width)
    term_list = []
    for section_index in range(section_count):
        contrib = backward_tiles(
            adjacency[0, 0, section_index],
            tile_coords[0, 0, section_index],
            tile_counts[0, 0, section_index],
            grad_tiles,
        )
        term_list.append(contrib.reshape(block_rows, feat_width))
    term_rows = jnp.stack(term_list, axis=0)
    shared_rows = lax.psum_scatter(term_rows, "rows", scatter_dimension=1, tiled=True)
    grad_inputs = shared_rows.astype(jnp.bfloat16)[None]
    return (hidden, grad_inputs, weight_total * scale_factor, bias_total * scale_factor)


def solution(mesh):
    return jax.shard_map(
        shards,
        mesh=mesh,
        in_specs=(
            P("rows", None),
            P("rows", "rep", None, None, None, None),
            P("rows", "rep", None, None, None),
            P("rows", "rep", None),
            P(),
            P(),
            P(("rows", "rep"), None),
        ),
        out_specs=(P(("rows", "rep"), None), P("rep", None, "rows", None), P(), P()),
        check_vma=False,
    )
```

profile of v0, /device:TPU:4, one launch (start us, length us, event | category | flops | bytes accessed | tf_op | source)
XLA Modules:
  0.0 1582.8 jit_solution(11975938991379185092)
XLA Ops:
  8.1 2.1 broadcast_select_fusion.1
  12.8 606.4 %all-reduce.7.cloned.1.call-done = (bf16[8,256,128]{2,1,0:T(8,128)(2,1)}, bf16[8,256,128]{2,1,0:T(8,128)(2,1)}) async-done(((bf16[8,256,128]{2,1,0:T(8,128)(2,1)}, bf16[8,256,128]{2,1,0:T(8,128)(2,1)}), (bf16[8,256,128]{2,1,0:T(8,128)(2,1)}, bf16[8,256,128]{2,1,0:T(8,128)(2,1)})) %all-reduce.7.cloned.1.call-update) | async-done | bytes 1048592 | tf_op jit(solution)/shard_map/psum | solution.py:11
  619.3 2.1 gather_fusion.1
  621.4 6.7 fusion.8
  628.1 6.3 copy.15
  634.4 2.6 gather_fusion
  637.0 7.6 fusion.14
  644.6 1.8 fusion.4
  646.4 6.3 copy.14
  652.7 4.3 fusion.29
  657.2 29.8 %all-reduce.8 = bf16[2048,128]{1,0:T(8,128)(2,1)S(1)} all-reduce(f32[2048,128]{1,0:T(8,128)S(1)} %bitcast.84), channel_id=1, replica_groups=mesh['rows'=64,'rep'=4] {'rep'}, use_global_device_ids=true, to_apply=%region_2.3 | all-reduce | flops 262144 | bytes 1572864 | tf_op jit(solution)/shard_map/psum | solution.py:62
  687.1 5.0 fusion.62
  694.6 5.8 fusion.6
  700.4 6.3 copy.17
  706.7 4.3 fusion
  713.2 5.8 fusion.12
  719.1 6.3 copy.16
  725.4 4.3 fusion.2
  730.9 1.5 pad_maximum_fusion
  732.4 152.5 %psum.39 = f32[256]{0:T(256)S(1)} all-reduce(f32[256]{0:T(256)S(1)} %get-tuple-element.6), channel_id=1, replica_groups=mesh['rows'=64,'rep'=4] {'rows'}, use_global_device_ids=true, to_apply=%region_6.7 | all-reduce | flops 256 | bytes 2048 | tf_op jit(solution)/shard_map/psum | solution.py:73
  884.9 2.0 fusion.32
  887.4 370.4 %all-reduce.5.cloned.1.call-done = f32[128,256]{1,0:T(8,128)} async-done(((f32[128,256]{1,0:T(8,128)}), f32[128,256]{1,0:T(8,128)}) %all-reduce.5.cloned.1.call-update) | async-done | bytes 131088 | tf_op jit(solution)/shard_map/psum | solution.py:73
  1257.8 1.6 broadcast_multiply_fusion
  1259.4 315.0 %reduce-scatter.2.cloned.1.call-done = f32[2,32,128]{2,1,0:T(8,128)} async-done(((f32[2,2048,128]{2,1,0:T(8,128)}), f32[2,32,128]{2,1,0:T(8,128)}) %reduce-scatter.2.cloned.1.call-update) | async-done | bytes 32784 | tf_op jit(solution)/shard_map/reduce_scatter | solution.py:89
  (44 shorter events, 10.7 us)
Async XLA Ops:
  8.0 679.0 %copy-start = (bf16[128,256]{1,0:T(8,128)(2,1)S(1)}, bf16[128,256]{1,0:T(8,128)(2,1)}, u32[]{:S(2)}) copy-start(bf16[128,256]{1,0:T(8,128)(2,1)} %param.11) | copy-start | bytes 196612
  8.0 2.8 copy-start.4
  8.0 2.9 copy-start.5
  8.0 611.2 %all-reduce.7.cloned.1.call-start = ((), (), s32[]{:S(2)}) async-start(), calls=%async_computation.4 | async-start | bytes 2097152 | tf_op jit(solution)/shard_map/psum | solution.py:11
  10.2 676.8 %all-gather.2.cloned.1.call-start = ((), (), s32[]{:S(2)}) async-start(), calls=%async_computation.1 | async-start | bytes 1310720 | tf_op jit(solution)/shard_map/all_gather | solution.py:65
  10.8 1247.0 %all-reduce.5.cloned.1.call-start = ((), (), s32[]{:S(2)}) async-start(), calls=%async_computation.3 | async-start | bytes 262144 | tf_op jit(solution)/shard_map/psum | solution.py:73
  628.1 6.3 copy-start.2
  634.4 10.2 slice-start
  637.0 7.6 slice-start.1
  657.0 30.0 %copy-start.6 = (f32[256]{0:T(256)S(1)}, f32[256]{0:T(256)}, u32[]{:S(2)}) copy-start(f32[256]{0:T(256)} %param.12) | copy-start | bytes 3076
  729.6 1.2 copy-start.3
  729.9 844.4 %reduce-scatter.2.cloned.1.call-start = ((), (), s32[]{:S(2)}) async-start(), calls=%async_computation.2 | async-start | bytes 2129920 | tf_op jit(solution)/shard_map/reduce_scatter | solution.py:89
  730.9 844.8 %copy-start.1 = (bf16[128,256]{1,0:T(8,128)(2,1)S(1)}, bf16[128,256]{1,0:T(8,128)(2,1)}, u32[]{:S(2)}) copy-start(bf16[128,256]{1,0:T(8,128)(2,1)} %param.11) | copy-start | bytes 196612
Sparse Core Ops, SparseCore 0:
  11.5 607.6 all-reduce.6
  730.0 527.7 all-reduce.4
  1260.3 314.0 reduce-scatter.1
Sparse Core Ops, SparseCore 1:
  12.5 26.1 all-gather.1
where the time goes:
time: 1590 us; the launch traced here: 1580 us
  waiting for transfers between devices  1290 us (81%)
  blocking collectives  182 us (11%)
  matrix products  47.2 us (3%)
  local copies, waits for them, and re-layouts  35.1 us (2%)
    psum x1, waiting for transfers between devices, spread(): return lax.psum(jnp.where(mine, value, jnp.zeros_like(value)), axis)  606 us
    psum x1, waiting for transfers between devices, shards(): weight_total, bias_total = lax.psum((weight_term, bias_term), 'rows')  370 us
    reduce_scatter x1, waiting for transfers between devices, shards(): lax.psum_scatter(term_rows, 'rows', scatter_dimension=1, tiled=True)  315 us
    psum x1, blocking collectives, shards(): weight_total, bias_total = lax.psum((weight_term, bias_term), 'rows')  152 us
  transfers between devices with their start and end apart: 4, of which 3 were waited for; matrix products, arithmetic and copies ran while one was open for 3% of the time, Pallas kernels for 0%

commit v1 on v0

v1 whole, which is shorter than its diff:
```python
import functools
import math

import jax
import jax.numpy as jnp
from jax import lax
from jax.experimental import pallas as pl
from jax.experimental.pallas import tpu as pltpu
from jax.sharding import PartitionSpec as P

MESH = pl.DeviceIdType.MESH
F32 = jnp.float32
BF16 = jnp.bfloat16
SLOTS = 80
XY_ORDER = (1, 3, 4, 5, 7, 2, 6)


def mm(a, b):
    return lax.dot_general(a, b, (((1,), (0,)), ((), ())), preferred_element_type=F32)


def mm_nt(a, b):
    return lax.dot_general(a, b, (((1,), (1,)), ((), ())), preferred_element_type=F32)


def mm_tn(a, b):
    return lax.dot_general(a, b, (((0,), (0,)), ((), ())), preferred_element_type=F32)


def arrived(ref, sem):
    pltpu.make_async_copy(ref, ref, sem).wait()


def kernel(
    scale,
    feat_hbm, adj_hbm, tab, w_ref, b_ref, cot_ref,
    hid_ref, gin_ref, gw_ref, gb_ref,
    adj, feat, acc, ps, pr, rt, acct, xs, xr, zs, zr, wa_s, wa, wb, wc,
    adj_sem, s1, s2, s3, r12, r3, ps_s, ps_r, rt_s, rt_r,
    wa_ss, wa_rs, wb_ss, wb_rs, wc_ss, wc_rs, xs_s, xs_r, zs_s, zs_r,
):
    row = lax.axis_index("rows")
    rep = lax.axis_index("rep")
    x = lax.rem(row, 4)
    z = lax.rem(lax.div(row, 4), 8)
    yl = lax.div(row, 32)
    yh = lax.div(rep, 2)
    core = lax.rem(rep, 2)

    def device(x, yl, z, yh, core):
        return (yl * 32 + z * 4 + x, yh * 2 + core)

    def xy_at(k, sign=1):
        return lax.rem(x + sign * (k % 4) + 4, 4), lax.rem(yl + k // 4, 2)

    def xy_peer(k):
        px, pyl = xy_at(k)
        return device(px, pyl, z, yh, core)

    def z_peer(k):
        return device(x, yl, lax.rem(z + k, 8), yh, core)

    def rep_peer(k):
        return device(x, yl, z, lax.rem(yh + k // 2, 2), lax.rem(core + k % 2, 2))

    a_pos = z * 2 + core
    b_pos = (yh * 2 + yl) * 4 + x

    def a_at(k):
        return lax.rem(a_pos + k, 16)

    def a_peer(k):
        pos = a_at(k)
        return device(x, yl, lax.div(pos, 2), yh, lax.rem(pos, 2))

    def b_peer(k):
        pos = lax.rem(b_pos + k, 16)
        py = lax.div(pos, 4)
        return device(lax.rem(pos, 4), lax.rem(py, 2), z, lax.div(py, 2), core)

    def send(src, dst, send_sem, recv_sem, peer):
        return pltpu.make_async_remote_copy(
            src_ref=src, dst_ref=dst, send_sem=send_sem, recv_sem=recv_sem,
            device_id=peer, device_id_type=MESH,
        )

    part = SLOTS // 4
    for i in range(4):
        pltpu.make_async_copy(
            adj_hbm.at[pl.ds(i * part, part)], adj.at[pl.ds(i * part, part)], adj_sem.at[i]
        ).start()

    barrier = pltpu.get_barrier_semaphore()
    greet = [xy_peer(k) for k in range(1, 8)]
    greet += [rep_peer(k) for k in range(1, 4)]
    greet += [a_peer(k) for k in range(1, 16)]
    for k in range(8):
        px, pyl = xy_at(k)
        if k > 0:
            greet.append(device(px, pyl, z, lax.rem(yh + 1, 2), core))
    for peer in greet:
        pl.semaphore_signal(barrier, inc=1, device_id=peer, device_id_type=MESH)
    pl.semaphore_wait(barrier, len(greet))

    my_j = yl * 4 + x
    is_root = [row == (rep * 2 + s) * 8 for s in range(2)]
    in_plane = [z == core * 4 + s * 2 for s in range(2)]

    def root_copy(s, k):
        px, pyl = xy_at(k)
        j = pyl * 4 + px
        return send(
            feat_hbm.at[pl.ds(pl.multiple_of(j * 256, 256), 256)], feat.at[s, j],
            s1.at[s, k], r12.at[s], device(px, pyl, z, yh, core),
        )

    def plane_copy(s, k):
        return send(feat.at[s, my_j], feat.at[s, my_j], s2.at[s, k], r12.at[s], z_peer(k))

    def side_copy(s, k):
        return send(feat.at[s, my_j], feat.at[s, my_j], s3.at[s, k], r3.at[s, k], xy_peer(k))

    for s in range(2):
        @pl.when(is_root[s])
        def _():
            for k in XY_ORDER:
                root_copy(s, k).start()
            pltpu.make_async_copy(
                feat_hbm.at[pl.ds(pl.multiple_of(my_j * 256, 256), 256)], feat.at[s, my_j], r12.at[s]
            ).start()

    acc[...] = jnp.zeros_like(acc)
    adj[SLOTS] = jnp.zeros((256, 256), BF16)

    for s in range(2):
        arrived(feat.at[s, my_j], r12.at[s])

        @pl.when(in_plane[s])
        def _():
            for k in (4, 3, 5, 2, 6, 1, 7):
                plane_copy(s, k).start()

        for k in XY_ORDER:
            side_copy(s, k).start()

    for i in range(4):
        view = adj.at[pl.ds(i * part, part)]
        arrived(view, adj_sem.at[i])

    def forward(i, carry):
        s = lax.div(i, 8)
        k = lax.rem(i, 8)
        fx = lax.rem(x - lax.rem(k, 4) + 4, 4)
        fyl = lax.rem(yl + lax.div(k, 4), 2)
        j = fyl * 4 + fx

        @pl.when(k > 0)
        def _():
            arrived(feat.at[s, j], r3.at[s, k])

        column = feat[s, j]
        for p in range(8):
            acc[p] += mm(adj[tab[s * 64 + p * 8 + j]], column)
        return carry

    lax.fori_loop(0, 16, forward, 0)

    def part_copy(k):
        return send(ps.at[k], pr.at[k], ps_s.at[k], ps_r.at[k], rep_peer(k))

    for k in (3, 2, 1):
        target = lax.rem(yh + k // 2, 2) * 2 + lax.rem(core + k % 2, 2)
        for h in range(2):
            ps[k, pl.ds(h * 256, 256)] = acc[target * 2 + h].astype(BF16)
        part_copy(k).start()
    for k in (1, 2, 3):
        arrived(pr.at[k], ps_r.at[k])

    c0 = math.sqrt(2.0 / math.pi)
    weight = w_ref[...]

    def epilogue(h, carry):
        wsum, bsum = carry
        rows = pl.ds(pl.multiple_of(h * 256, 256), 256)
        total = acc[rep * 2 + h] + pr[1, rows].astype(F32)
        total += pr[2, rows].astype(F32)
        total += pr[3, rows].astype(F32)
        agg = total.astype(BF16)
        v = mm(agg, weight) + b_ref[...]
        v2 = v * v
        t = jnp.tanh(c0 * (v + 0.044715 * (v2 * v)))
        half = 0.5 * (1.0 + t)
        hid_ref[rows] = (v * half).astype(BF16)
        slope = half + 0.5 * v * (1.0 - t * t) * (c0 * (1.0 + 0.134145 * v2))
        grad = cot_ref[rows].astype(F32) * slope
        grad_bf = grad.astype(BF16)
        rt[rep, :, rows] = mm_nt(weight, grad_bf).astype(BF16)
        wsum = wsum + mm_tn(agg, grad_bf)
        bsum = bsum + jnp.sum(grad.reshape(32, 8, 256), axis=0)
        return wsum, bsum

    carry = (jnp.zeros((128, 256), F32), jnp.zeros((8, 256), F32))
    for h in range(2):
        carry = epilogue(h, carry)
    wsum, bsum = carry

    def rows_copy(k):
        return send(rt.at[rep], rt.at[rep], rt_s.at[k], rt_r.at[k], rep_peer(k))

    for k in (3, 2, 1):
        rows_copy(k).start()

    for j in range(16):
        wa_s[j, pl.ds(0, 8)] = wsum[j * 8 : j * 8 + 8]
        wa_s[j, pl.ds(8, 8)] = bsum

    def wa_copy(k):
        return send(wa_s.at[a_at(k)], wa.at[a_pos], wa_ss.at[k], wa_rs.at[k], a_peer(k))

    for k in range(1, 16):
        wa_copy(k).start()
    wa[a_pos] = wa_s[a_pos]

    def quarter_of(k):
        return lax.rem(yh + k // 2, 2) * 2 + lax.rem(core + k % 2, 2)

    def back_terms(s, q, quarter):
        left = rt[quarter]
        out = mm(left[:, :256], adj[tab[s * 64 + quarter * 16 + q]])
        return out + mm(left[:, 256:], adj[tab[s * 64 + quarter * 16 + 8 + q]])

    def back_own(i, carry):
        s, q = lax.div(i, 8), lax.rem(i, 8)
        acct[s, q] = back_terms(s, q, quarter_of(0))
        return carry

    lax.fori_loop(0, 16, back_own, 0)
    arrived(rt.at[quarter_of(1)], rt_r.at[1])

    def back_core(i, carry):
        s, q = lax.div(i, 8), lax.rem(i, 8)
        acct[s, q] += back_terms(s, q, quarter_of(1))
        return carry

    lax.fori_loop(0, 16, back_core, 0)
    for k in (2, 3):
        arrived(rt.at[quarter_of(k)], rt_r.at[k])

    def xs_copy(s, k):
        px, pyl = xy_at(k)
        return send(xs.at[s, pyl * 4 + px], xr.at[s, k], xs_s.at[s, k], xs_r.at[s, k], xy_peer(k))

    for hk in (1, 0):
        half = lax.rem(yl + hk, 2)
        for s in range(2):
            def back_rest(zz, carry):
                q = half * 4 + zz
                total = acct[s, q] + back_terms(s, q, quarter_of(2))
                total += back_terms(s, q, quarter_of(3))
                out = total.T.astype(BF16)
                for zl in range(2):
                    for px in range(4):
                        at = zl * 128 + px * 32
                        xs[s, half * 4 + px, zz * 2 + zl] = out[at : at + 32]
                return carry

            lax.fori_loop(0, 4, back_rest, 0)
            for k in (1, 3, 2) if hk == 0 else (4, 5, 7, 6):
                xs_copy(s, k).start()

    for k in range(1, 16):
        arrived(wa.at[lax.rem(a_pos - k + 16, 16)], wa_rs.at[k])
    total = wa[0]
    for j in range(1, 16):
        total = total + wa[j]
    wb[b_pos] = total

    def wb_copy(k):
        return send(wb.at[b_pos], wb.at[b_pos], wb_ss.at[k], wb_rs.at[k], b_peer(k))

    for k in range(1, 16):
        wb_copy(k).start()

    def zs_copy(s, k):
        return send(zs.at[s, lax.rem(z + k, 8)], zr.at[s, k], zs_s.at[s, k], zs_r.at[s, k], z_peer(k))

    for s in range(2):
        for k in range(1, 8):
            arrived(xr.at[s, k], xs_r.at[s, k])
        for zz in range(8):
            total = xs[s, my_j, zz].astype(F32)
            for k in range(1, 8):
                total += xr[s, k, zz].astype(F32)
            zs[s, zz] = total.astype(BF16)
        for k in (4, 3, 5, 2, 6, 1, 7):
            zs_copy(s, k).start()

    for k in range(1, 16):
        arrived(wb.at[lax.rem(b_pos - k + 16, 16)], wb_rs.at[k])
    total = wb[0]
    for j in range(1, 16):
        total = total + wb[j]
    wc[a_pos] = total[:8] * scale
    gb_ref[...] = jnp.sum(total[8:], axis=0, keepdims=True) * scale

    def wc_copy(k):
        return send(wc.at[a_pos], wc.at[a_pos], wc_ss.at[k], wc_rs.at[k], a_peer(k))

    for k in range(1, 16):
        wc_copy(k).start()

    for s in range(2):
        total = zs[s, z].astype(F32)
        for k in range(1, 8):
            arrived(zr.at[s, k], zs_r.at[s, k])
            total += zr[s, k].astype(F32)
        gin_ref[s] = total.astype(BF16)

    for k in range(1, 16):
        arrived(wc.at[lax.rem(a_pos - k + 16, 16)], wc_rs.at[k])
    gw_ref[...] = wc[...]

    for s in range(2):
        @pl.when(is_root[s])
        def _():
            for k in range(1, 8):
                root_copy(s, k).wait_send()

        @pl.when(in_plane[s])
        def _():
            for k in range(1, 8):
                plane_copy(s, k).wait_send()

        for k in range(1, 8):
            side_copy(s, k).wait_send()
            xs_copy(s, k).wait_send()
            zs_copy(s, k).wait_send()
    for k in range(1, 4):
        part_copy(k).wait_send()
        rows_copy(k).wait_send()
    for k in range(1, 16):
        wa_copy(k).wait_send()
        wb_copy(k).wait_send()
        wc_copy(k).wait_send()


def layer(features, adjacency, table, weight, bias, cotangent, scale):
    vmem = pl.BlockSpec(memory_space=pltpu.VMEM)
    hbm = pl.BlockSpec(memory_space=pl.ANY)
    sems = [
        (4,), (2, 8), (2, 8), (2, 8), (2,), (2, 8), (4,), (4,), (4,), (4,),
        (16,), (16,), (16,), (16,), (16,), (16,), (2, 8), (2, 8), (2, 8), (2, 8),
    ]
    return pl.pallas_call(
        functools.partial(kernel, scale),
        name="layer",
        out_shape=(
            jax.ShapeDtypeStruct((512, 256), BF16),
            jax.ShapeDtypeStruct((2, 32, 128), BF16),
            jax.ShapeDtypeStruct((16, 8, 256), F32),
            jax.ShapeDtypeStruct((1, 256), F32),
        ),
        in_specs=[hbm, hbm, pl.BlockSpec(memory_space=pltpu.SMEM), vmem, vmem, vmem],
        out_specs=(vmem, vmem, vmem, vmem),
        scratch_shapes=[
            pltpu.VMEM((SLOTS + 1, 256, 256), BF16),
            pltpu.VMEM((2, 8, 256, 128), BF16),
            pltpu.VMEM((8, 256, 128), F32),
            pltpu.VMEM((4, 512, 128), BF16),
            pltpu.VMEM((4, 512, 128), BF16),
            pltpu.VMEM((4, 128, 512), BF16),
            pltpu.VMEM((2, 8, 128, 256), F32),
            pltpu.VMEM((2, 8, 8, 32, 128), BF16),
            pltpu.VMEM((2, 8, 8, 32, 128), BF16),
            pltpu.VMEM((2, 8, 32, 128), BF16),
            pltpu.VMEM((2, 8, 32, 128), BF16),
            pltpu.VMEM((16, 16, 256), F32),
            pltpu.VMEM((16, 16, 256), F32),
            pltpu.VMEM((16, 16, 256), F32),
            pltpu.VMEM((16, 8, 256), F32),
        ]
        + [pltpu.SemaphoreType.DMA(shape) for shape in sems],
        compiler_params=pltpu.CompilerParams(
            collective_id=1, has_side_effects=True, vmem_limit_bytes=40 * 2**20
        ),
    )(features, adjacency, table, weight, bias, cotangent)


def shards(features, adjacency, tile_coords, tile_counts, weight, bias, cotangent):
    rows_count = lax.axis_size("rows")
    scale = 1.0 / math.sqrt(features.shape[0] * rows_count)
    coords = tile_coords[0, 0]
    counts = tile_counts[0, 0]
    slot = jnp.arange(40, dtype=jnp.int32)
    place = jnp.where(slot[None, :] < counts[:, None], coords[:, 0] * 8 + coords[:, 1], -1)
    hit = place[:, None, :] == jnp.arange(64, dtype=jnp.int32)[None, :, None]
    number = slot[None, None, :] + 40 * jnp.arange(2, dtype=jnp.int32)[:, None, None] - SLOTS
    table = SLOTS + jnp.sum(jnp.where(hit, number, 0), axis=2)
    hidden, grad_inputs, grad_weight, grad_bias = layer(
        features,
        adjacency.reshape(SLOTS, 256, 256),
        table.reshape(128),
        weight,
        bias.reshape(1, 256),
        cotangent,
        scale,
    )
    return hidden, grad_inputs[None], grad_weight.reshape(128, 256), grad_bias.reshape(256)


def solution(mesh):
    return jax.shard_map(
        shards,
        mesh=mesh,
        in_specs=(
            P("rows", None),
            P("rows", "rep", None, None, None, None),
            P("rows", "rep", None, None, None),
            P("rows", "rep", None),
            P(),
            P(),
            P(("rows", "rep"), None),
        ),
        out_specs=(P(("rows", "rep"), None), P("rep", None, "rows", None), P(), P()),
        check_vma=False,
    )
```

time: 1590 us -> 89.7 us (0.06)
  waiting for transfers between devices: 1290 us -> 0 us
  blocking collectives: 182 us -> 0 us
  Pallas kernels: 0 us -> 77.3 us
  matrix products: 47.2 us -> 0 us
  local copies, waits for them, and re-layouts: 35.1 us -> 10.1 us
    psum x2 -> x0, waiting for transfers between devices: 977 us -> none  [the longest x1 606 us: spread(): return lax.psum(jnp.where(mine, value, jnp.zeros_like(value)), axis)]
    reduce_scatter x1 -> x0, waiting for transfers between devices: 315 us -> none  [shards(): lax.psum_scatter(term_rows, 'rows', scatter_dimension=1, tiled=True)]
    psum x2 -> x0, blocking collectives: 182 us -> none  [the longest x1 152 us: shards(): weight_total, bias_total = lax.psum((weight_term, bias_term), 'rows')]
    pallas_call x0 -> x1, Pallas kernels: none -> 77.3 us  [layer(): pl.pallas_call(functools.partial(kernel, scale), name='layer', out_shape=...]
    dot_general x11 -> x0, matrix products: 47.2 us -> none  [the longest x2 14.3 us: forward_tiles(): jnp.einsum('tij,tjf->tif', tile_values, chosen, preferred_element_type=jn...]
    dot_general x6 -> x0, local copies, waits for them, and re-layouts: 26.6 us -> none  [the longest x2 12.6 us: forward_tiles(): jnp.einsum('tij,tjf->tif', tile_values, chosen, preferred_element_type=jn...]
  transfers between devices with their start and end apart: 4 -> 0, of which waited for: 3 -> 0; matrix products, arithmetic and copies ran while one was open for 3% -> 0% of each run, Pallas kernels for 0% -> 0%
where the time goes in v1:
time: 89.7 us; the launch traced here: 89.1 us
  Pallas kernels  77.3 us (86%)
  local copies, waits for them, and re-layouts  10.1 us (11%)
  other arithmetic  1.01 us (1%)
    pallas_call x1, Pallas kernels, layer(): pl.pallas_call(functools.partial(kernel, scale), name='layer', out_shape=...  77.3 us
    unnamed x14, local copies, waits for them, and re-layouts  10 us

profile of v1, /device:TPU:4, one launch (start us, length us, event | category | flops | bytes accessed | tf_op | source)
XLA Modules:
  0.0 89.1 jit_solution(7733436467177758795)
XLA Ops:
  0.6 0.1 add_add_fusion
  0.7 0.8 compare_select_fusion
  1.5 0.1 select_reduce_fusion
  1.7 0.1 add.44.tab
  1.7 0.0 copy-start
  1.7 4.0 %copy-done = bf16[1,1,2,40,256,256]{5,4,3,2,1,0:T(8,128)(2,1)S(1)} copy-done((bf16[1,1,2,40,256,256]{5,4,3,2,1,0:T(8,128)(2,1)S(1)}, bf16[1,1,2,40,256,256]{5,4,3,2,1,0:T(8,128)(2,1)}, u32[]{:S(2)}) %copy-start) | copy-done | bytes 10485784
  5.7 0.0 copy-start.1
  5.7 1.0 %copy-done.1 = bf16[2048,128]{1,0:T(8,128)(2,1)S(1)} copy-done((bf16[2048,128]{1,0:T(8,128)(2,1)S(1)}, bf16[2048,128]{1,0:T(8,128)(2,1)}, u32[]{:S(2)}) %copy-start.1) | copy-done | bytes 524312
  6.8 0.0 copy-start.2
  6.8 0.9 %copy-done.2 = bf16[512,256]{1,0:T(8,128)(2,1)S(1)} copy-done((bf16[512,256]{1,0:T(8,128)(2,1)S(1)}, bf16[512,256]{1,0:T(8,128)(2,1)}, u32[]{:S(2)}) %copy-start.2) | copy-done | bytes 262168
  7.7 0.0 copy-start.3
  7.7 0.8 copy-done.3
  8.6 0.0 copy-start.4
  8.6 0.7 copy-done.4
  9.3 77.3 %layer.1 = (bf16[512,256]{1,0:T(8,128)(2,1)S(1)}, bf16[2,32,128]{2,1,0:T(8,128)(2,1)S(1)}, f32[16,8,256]{2,1,0:T(8,128)S(1)}, f32[1,256]{1,0:T(1,128)S(1)}) custom-call(bf16[2048,128]{1,0:T(8,128)(2,1)S(1)} %copy-done.1, bf16[80,256,256]{2,1,0:T(8,128)(2,1)S(1)} %bitcast.8, s32[128]{0:T(128)S(1)} %add.44.tab, bf16[128,256]{1,0:T(8,128)(2,1)S(1)} %copy-done.3, ...), custom_call_target="tpu_custom_call" | custom-call | tf_op jit(solution)/shard_map/layer/pallas_call | solution.py:354
  86.6 0.7 copy.15
  87.3 0.6 copy.16
  87.9 0.7 copy.17
  88.6 0.6 copy.18
  (2 shorter events, 0.0 us)
Async XLA Ops:
  1.7 4.0 %copy-start = (bf16[1,1,2,40,256,256]{5,4,3,2,1,0:T(8,128)(2,1)S(1)}, bf16[1,1,2,40,256,256]{5,4,3,2,1,0:T(8,128)(2,1)}, u32[]{:S(2)}) copy-start(bf16[1,1,2,40,256,256]{5,4,3,2,1,0:T(8,128)(2,1)} %param.8) | copy-start | bytes 31457284
  5.7 1.0 %copy-start.1 = (bf16[2048,128]{1,0:T(8,128)(2,1)S(1)}, bf16[2048,128]{1,0:T(8,128)(2,1)}, u32[]{:S(2)}) copy-start(bf16[2048,128]{1,0:T(8,128)(2,1)} %feat_hbm.1) | copy-start | bytes 1572868
  6.8 0.9 %copy-start.2 = (bf16[512,256]{1,0:T(8,128)(2,1)S(1)}, bf16[512,256]{1,0:T(8,128)(2,1)}, u32[]{:S(2)}) copy-start(bf16[512,256]{1,0:T(8,128)(2,1)} %cot_ref.1) | copy-start | bytes 786436
  7.7 0.8 copy-start.3
  8.6 0.7 copy-start.4

commit v2 on v1

--- a/solution.py
+++ b/solution.py
@@ -12,6 +12,7 @@
 F32 = jnp.float32
 BF16 = jnp.bfloat16
 SLOTS = 80
+VMEM_BYTES = 62 * 2**20
 XY_ORDER = (1, 3, 4, 5, 7, 2, 6)
 
 
@@ -33,11 +34,13 @@
 
 def kernel(
     scale,
-    feat_hbm, adj_hbm, tab, w_ref, b_ref, cot_ref,
-    hid_ref, gin_ref, gw_ref, gb_ref,
-    adj, feat, acc, ps, pr, rt, acct, xs, xr, zs, zr, wa_s, wa, wb, wc,
-    adj_sem, s1, s2, s3, r12, r3, ps_s, ps_r, rt_s, rt_r,
-    wa_ss, wa_rs, wb_ss, wb_rs, wc_ss, wc_rs, xs_s, xs_r, zs_s, zs_r,
+    feat_hbm, adj_hbm, tab, w_hbm, b_hbm, cot_hbm,
+    hid_hbm, gin_hbm, gw_hbm, gb_hbm,
+    adj, feat, acc, pf, ps, pr, rt, acct, xs, xr, zs, zr,
+    w_ref, b_ref, cot_ref, hid_ref, gin_ref, gb_ref, wa_s, wa, wb, wc, ba_s, ba, bb, bc,
+    adj_sem, in_sem, out_sem, s1, s2, s3, r12, r3, ps_s, ps_r, rt_s, rt_r,
+    wa_ss, wa_rs, wb_ss, wb_rs, wc_ss, wc_rs,
+    ba_ss, ba_rs, bb_ss, bb_rs, bc_ss, bc_rs, xs_s, xs_r, zs_s, zs_r,
 ):
     row = lax.axis_index("rows")
     rep = lax.axis_index("rep")
@@ -63,20 +66,20 @@
     def rep_peer(k):
         return device(x, yl, z, lax.rem(yh + k // 2, 2), lax.rem(core + k % 2, 2))
 
-    a_pos = z * 2 + core
-    b_pos = (yh * 2 + yl) * 4 + x
+    a_pos = (yh * 2 + yl) * 4 + x
+    b_pos = z * 2 + core
 
     def a_at(k):
         return lax.rem(a_pos + k, 16)
 
     def a_peer(k):
         pos = a_at(k)
-        return device(x, yl, lax.div(pos, 2), yh, lax.rem(pos, 2))
+        py = lax.div(pos, 4)
+        return device(lax.rem(pos, 4), lax.rem(py, 2), z, lax.div(py, 2), core)
 
     def b_peer(k):
         pos = lax.rem(b_pos + k, 16)
-        py = lax.div(pos, 4)
-        return device(lax.rem(pos, 4), lax.rem(py, 2), z, lax.div(py, 2), core)
+        return device(x, yl, lax.div(pos, 2), yh, lax.rem(pos, 2))
 
     def send(src, dst, send_sem, recv_sem, peer):
         return pltpu.make_async_remote_copy(
@@ -84,20 +87,22 @@
             device_id=peer, device_id_type=MESH,
         )
 
+    sent = []
+
     part = SLOTS // 4
     for i in range(4):
         pltpu.make_async_copy(
             adj_hbm.at[pl.ds(i * part, part)], adj.at[pl.ds(i * part, part)], adj_sem.at[i]
         ).start()
 
+    small = [(w_hbm, w_ref), (b_hbm, b_ref), (cot_hbm, cot_ref)]
+    for i, (src, dst) in enumerate(small):
+        pltpu.make_async_copy(src, dst, in_sem.at[i]).start()
+
     barrier = pltpu.get_barrier_semaphore()
-    greet = [xy_peer(k) for k in range(1, 8)]
-    greet += [rep_peer(k) for k in range(1, 4)]
-    greet += [a_peer(k) for k in range(1, 16)]
-    for k in range(8):
-        px, pyl = xy_at(k)
-        if k > 0:
-            greet.append(device(px, pyl, z, lax.rem(yh + 1, 2), core))
+    greet = [a_peer(k) for k in range(1, 16)]
+    greet += [b_peer(k) for k in range(1, 16)]
+    greet.append(rep_peer(3))
     for peer in greet:
         pl.semaphore_signal(barrier, inc=1, device_id=peer, device_id_type=MESH)
     pl.semaphore_wait(barrier, len(greet))
@@ -120,6 +125,12 @@
     def side_copy(s, k):
         return send(feat.at[s, my_j], feat.at[s, my_j], s3.at[s, k], r3.at[s, k], xy_peer(k))
 
+    def drain_if(cond, copy, s):
+        @pl.when(cond)
+        def _():
+            for k in range(1, 8):
+                copy(s, k).wait_send()
+
     for s in range(2):
         @pl.when(is_root[s])
         def _():
@@ -129,6 +140,8 @@
                 feat_hbm.at[pl.ds(pl.multiple_of(my_j * 256, 256), 256)], feat.at[s, my_j], r12.at[s]
             ).start()
 
+        sent.append(functools.partial(drain_if, is_root[s], root_copy, s))
+
     acc[...] = jnp.zeros_like(acc)
     adj[SLOTS] = jnp.zeros((256, 256), BF16)
 
@@ -140,9 +153,14 @@
             for k in (4, 3, 5, 2, 6, 1, 7):
                 plane_copy(s, k).start()
 
+        sent.append(functools.partial(drain_if, in_plane[s], plane_copy, s))
+
         for k in XY_ORDER:
             side_copy(s, k).start()
-
+            sent.append(side_copy(s, k).wait_send)
+
+    for i, (src, dst) in enumerate(small):
+        arrived(dst, in_sem.at[i])
     for i in range(4):
         view = adj.at[pl.ds(i * part, part)]
         arrived(view, adj_sem.at[i])
@@ -165,16 +183,24 @@
 
     lax.fori_loop(0, 16, forward, 0)
 
-    def part_copy(k):
-        return send(ps.at[k], pr.at[k], ps_s.at[k], ps_r.at[k], rep_peer(k))
-
-    for k in (3, 2, 1):
-        target = lax.rem(yh + k // 2, 2) * 2 + lax.rem(core + k % 2, 2)
-        for h in range(2):
-            ps[k, pl.ds(h * 256, 256)] = acc[target * 2 + h].astype(BF16)
-        part_copy(k).start()
-    for k in (1, 2, 3):
-        arrived(pr.at[k], ps_r.at[k])
+    far_yh, other = lax.rem(yh + 1, 2), lax.rem(core + 1, 2)
+
+    def core_copy(i):
+        quarter = (far_yh, yh)[i] * 2 + other
+        return send(acc.at[pl.ds(quarter * 2, 2)], pf.at[i], ps_s.at[i], ps_r.at[i], rep_peer(1))
+
+    def far_copy(h):
+        return send(ps.at[h], pr.at[h], ps_s.at[2 + h], ps_r.at[2 + h], rep_peer(2))
+
+    for i in range(2):
+        core_copy(i).start()
+        sent.append(core_copy(i).wait_send)
+    arrived(pf.at[0], ps_r.at[0])
+    for h in range(2):
+        ps[h] = (acc[(far_yh * 2 + core) * 2 + h] + pf[0, h]).astype(BF16)
+        far_copy(h).start()
+        sent.append(far_copy(h).wait_send)
+    arrived(pf.at[1], ps_r.at[1])
 
     c0 = math.sqrt(2.0 / math.pi)
     weight = w_ref[...]
@@ -182,9 +208,9 @@
     def epilogue(h, carry):
         wsum, bsum = carry
         rows = pl.ds(pl.multiple_of(h * 256, 256), 256)
-        total = acc[rep * 2 + h] + pr[1, rows].astype(F32)
-        total += pr[2, rows].astype(F32)
-        total += pr[3, rows].astype(F32)
+        total = acc[rep * 2 + h] + pf[1, h]
+        arrived(pr.at[h], ps_r.at[2 + h])
+        total += pr[h].astype(F32)
         agg = total.astype(BF16)
         v = mm(agg, weight) + b_ref[...]
         v2 = v * v
@@ -204,22 +230,115 @@
         carry = epilogue(h, carry)
     wsum, bsum = carry
 
+    def put(i, src, dst):
+        copy = pltpu.make_async_copy(src, dst, out_sem.at[i])
+        copy.start()
+        sent.append(copy.wait)
+
     def rows_copy(k):
         return send(rt.at[rep], rt.at[rep], rt_s.at[k], rt_r.at[k], rep_peer(k))
 
-    for k in (3, 2, 1):
+    def pass_on():
+        far = rt.at[lax.rem(yh + 1, 2) * 2 + core]
+        return send(far, far, rt_s.at[3], rt_r.at[3], rep_peer(1))
+
+    for k in (2, 1):
         rows_copy(k).start()
+        sent.append(rows_copy(k).wait_send)
+
+    put(0, hid_ref, hid_hbm)
 
     for j in range(16):
-        wa_s[j, pl.ds(0, 8)] = wsum[j * 8 : j * 8 + 8]
-        wa_s[j, pl.ds(8, 8)] = bsum
+        wa_s[j] = wsum[j * 8 : j * 8 + 8]
+    ba_s[...] = bsum
+    first = a_pos == 0
 
     def wa_copy(k):
         return send(wa_s.at[a_at(k)], wa.at[a_pos], wa_ss.at[k], wa_rs.at[k], a_peer(k))
 
+    def ba_copy():
+        return send(ba_s, ba.at[a_pos], ba_ss, ba_rs.at[a_pos], device(0, 0, z, 0, core))
+
     for k in range(1, 16):
         wa_copy(k).start()
+        sent.append(wa_copy(k).wait_send)
     wa[a_pos] = wa_s[a_pos]
+
+    @pl.when(a_pos > 0)
+    def _():
+        ba_copy().start()
+
+    @pl.when(first)
+    def _():
+        ba[0] = bsum
+
+    def ba_drain():
+        @pl.when(a_pos > 0)
+        def _():
+            ba_copy().wait_send()
+
+    sent.append(ba_drain)
+
+    def wb_copy(k):
+        return send(wb.at[b_pos], wb.at[b_pos], wb_ss.at[k], wb_rs.at[k], b_peer(k))
+
+    def bb_copy(k):
+        return send(bb.at[b_pos], bb.at[b_pos], bb_ss.at[k], bb_rs.at[k], b_peer(k))
+
+    def add_up(ref):
+        total = ref[0]
+        for j in range(1, 16):
+            total = total + ref[j]
+        return total
+
+    def step_b():
+        for k in range(1, 16):
+            arrived(wa.at[lax.rem(a_pos - k + 16, 16)], wa_rs.at[k])
+        wb[b_pos] = add_up(wa)
+        for k in range(1, 16):
+            wb_copy(k).start()
+            sent.append(wb_copy(k).wait_send)
+
+        @pl.when(first)
+        def _():
+            for j in range(1, 16):
+                arrived(ba.at[j], ba_rs.at[j])
+            bb[b_pos] = add_up(ba)
+            for k in range(1, 16):
+                bb_copy(k).start()
+
+        sent.append(functools.partial(drain_first, bb_copy))
+
+    def drain_first(copy):
+        @pl.when(first)
+        def _():
+            for k in range(1, 16):
+                copy(k).wait_send()
+
+    def wc_copy(k):
+        return send(wc.at[a_pos], wc.at[a_pos], wc_ss.at[k], wc_rs.at[k], a_peer(k))
+
+    def bc_copy(k):
+        return send(bc, bc, bc_ss.at[k], bc_rs, a_peer(k))
+
+    def step_c():
+        for k in range(1, 16):
+            arrived(wb.at[lax.rem(b_pos - k + 16, 16)], wb_rs.at[k])
+        wc[a_pos] = add_up(wb) * scale
+        for k in range(1, 16):
+            wc_copy(k).start()
+            sent.append(wc_copy(k).wait_send)
+
+        @pl.when(first)
+        def _():
+            for k in range(1, 16):
+                arrived(bb.at[lax.rem(b_pos - k + 16, 16)], bb_rs.at[k])
+            total = jnp.sum(add_up(bb), axis=0, keepdims=True) * scale
+            bc[...] = jnp.broadcast_to(total, (8, 256))
+            for k in range(1, 16):
+                bc_copy(k).start()
+
+        sent.append(functools.partial(drain_first, bc_copy))
 
     def quarter_of(k):
         return lax.rem(yh + k // 2, 2) * 2 + lax.rem(core + k % 2, 2)
@@ -234,7 +353,7 @@
         acct[s, q] = back_terms(s, q, quarter_of(0))
         return carry
 
-    lax.fori_loop(0, 16, back_own, 0)
+    lax.fori_loop(0, 16, back_own, 0, unroll=4)
     arrived(rt.at[quarter_of(1)], rt_r.at[1])
 
     def back_core(i, carry):
@@ -242,21 +361,31 @@
         acct[s, q] += back_terms(s, q, quarter_of(1))
         return carry
 
-    lax.fori_loop(0, 16, back_core, 0)
-    for k in (2, 3):
-        arrived(rt.at[quarter_of(k)], rt_r.at[k])
+    lax.fori_loop(0, 16, back_core, 0, unroll=4)
+    arrived(rt.at[quarter_of(2)], rt_r.at[2])
+    pass_on().start()
+    sent.append(pass_on().wait_send)
+
+    def back_far(i, carry):
+        s, q = lax.div(i, 8), lax.rem(i, 8)
+        acct[s, q] += back_terms(s, q, quarter_of(2))
+        return carry
+
+    lax.fori_loop(0, 16, back_far, 0, unroll=4)
+    step_b()
+    arrived(rt.at[quarter_of(3)], rt_r.at[3])
 
     def xs_copy(s, k):
         px, pyl = xy_at(k)
         return send(xs.at[s, pyl * 4 + px], xr.at[s, k], xs_s.at[s, k], xs_r.at[s, k], xy_peer(k))
 
-    for hk in (1, 0):
-        half = lax.rem(yl + hk, 2)
-        for s in range(2):
+    for s in range(2):
+        for hk in (1, 0):
+            half = lax.rem(yl + hk, 2)
+
             def back_rest(zz, carry):
                 q = half * 4 + zz
-                total = acct[s, q] + back_terms(s, q, quarter_of(2))
-                total += back_terms(s, q, quarter_of(3))
+                total = acct[s, q] + back_terms(s, q, quarter_of(3))
                 out = total.T.astype(BF16)
                 for zl in range(2):
                     for px in range(4):
@@ -264,22 +393,12 @@
                         xs[s, half * 4 + px, zz * 2 + zl] = out[at : at + 32]
                 return carry
 
-            lax.fori_loop(0, 4, back_rest, 0)
+            lax.fori_loop(0, 4, back_rest, 0, unroll=True)
             for k in (1, 3, 2) if hk == 0 else (4, 5, 7, 6):
                 xs_copy(s, k).start()
-
-    for k in range(1, 16):
-        arrived(wa.at[lax.rem(a_pos - k + 16, 16)], wa_rs.at[k])
-    total = wa[0]
-    for j in range(1, 16):
-        total = total + wa[j]
-    wb[b_pos] = total
-
-    def wb_copy(k):
-        return send(wb.at[b_pos], wb.at[b_pos], wb_ss.at[k], wb_rs.at[k], b_peer(k))
-
-    for k in range(1, 16):
-        wb_copy(k).start()
+                sent.append(xs_copy(s, k).wait_send)
+
+    step_c()
 
     def zs_copy(s, k):
         return send(zs.at[s, lax.rem(z + k, 8)], zr.at[s, k], zs_s.at[s, k], zs_r.at[s, k], z_peer(k))
@@ -294,20 +413,7 @@
             zs[s, zz] = total.astype(BF16)
         for k in (4, 3, 5, 2, 6, 1, 7):
             zs_copy(s, k).start()
-
-    for k in range(1, 16):
-        arrived(wb.at[lax.rem(b_pos - k + 16, 16)], wb_rs.at[k])
-    total = wb[0]
-    for j in range(1, 16):
-        total = total + wb[j]
-    wc[a_pos] = total[:8] * scale
-    gb_ref[...] = jnp.sum(total[8:], axis=0, keepdims=True) * scale
-
-    def wc_copy(k):
-        return send(wc.at[a_pos], wc.at[a_pos], wc_ss.at[k], wc_rs.at[k], a_peer(k))
-
-    for k in range(1, 16):
-        wc_copy(k).start()
+            sent.append(zs_copy(s, k).wait_send)
 
     for s in range(2):
         total = zs[s, z].astype(F32)
@@ -315,41 +421,29 @@
             arrived(zr.at[s, k], zs_r.at[s, k])
             total += zr[s, k].astype(F32)
         gin_ref[s] = total.astype(BF16)
+    put(1, gin_ref, gin_hbm)
 
     for k in range(1, 16):
         arrived(wc.at[lax.rem(a_pos - k + 16, 16)], wc_rs.at[k])
-    gw_ref[...] = wc[...]
-
-    for s in range(2):
-        @pl.when(is_root[s])
-        def _():
-            for k in range(1, 8):
-                root_copy(s, k).wait_send()
-
-        @pl.when(in_plane[s])
-        def _():
-            for k in range(1, 8):
-                plane_copy(s, k).wait_send()
-
-        for k in range(1, 8):
-            side_copy(s, k).wait_send()
-            xs_copy(s, k).wait_send()
-            zs_copy(s, k).wait_send()
-    for k in range(1, 4):
-        part_copy(k).wait_send()
-        rows_copy(k).wait_send()
-    for k in range(1, 16):
-        wa_copy(k).wait_send()
-        wb_copy(k).wait_send()
-        wc_copy(k).wait_send()
+    put(2, wc, gw_hbm)
+
+    @pl.when(a_pos > 0)
+    def _():
+        arrived(bc, bc_rs)
+
+    gb_ref[...] = bc[pl.ds(0, 1)]
+    put(3, gb_ref, gb_hbm)
+
+    for drain in sent:
+        drain()
 
 
 def layer(features, adjacency, table, weight, bias, cotangent, scale):
-    vmem = pl.BlockSpec(memory_space=pltpu.VMEM)
-    hbm = pl.BlockSpec(memory_space=pl.ANY)
+    hbm = pl.BlockSpec(memory_space=pltpu.HBM)
     sems = [
-        (4,), (2, 8), (2, 8), (2, 8), (2,), (2, 8), (4,), (4,), (4,), (4,),
-        (16,), (16,), (16,), (16,), (16,), (16,), (2, 8), (2, 8), (2, 8), (2, 8),
+        (4,), (3,), (4,), (2, 8), (2, 8), (2, 8), (2,), (2, 8), (4,), (4,), (4,), (4,),
+        (16,), (16,), (16,), (16,), (16,), (16,), (), (16,), (16,), (16,), (16,), (),
+        (2, 8), (2, 8), (2, 8), (2, 8),
     ]
     return pl.pallas_call(
         functools.partial(kernel, scale),
@@ -360,30 +454,69 @@
             jax.ShapeDtypeStruct((16, 8, 256), F32),
             jax.ShapeDtypeStruct((1, 256), F32),
         ),
-        in_specs=[hbm, hbm, pl.BlockSpec(memory_space=pltpu.SMEM), vmem, vmem, vmem],
-        out_specs=(vmem, vmem, vmem, vmem),
+        in_specs=[hbm, hbm, pl.BlockSpec(memory_space=pltpu.SMEM), hbm, hbm, hbm],
+        out_specs=(hbm, hbm, hbm, hbm),
         scratch_shapes=[
             pltpu.VMEM((SLOTS + 1, 256, 256), BF16),
             pltpu.VMEM((2, 8, 256, 128), BF16),
             pltpu.VMEM((8, 256, 128), F32),
-            pltpu.VMEM((4, 512, 128), BF16),
-            pltpu.VMEM((4, 512, 128), BF16),
+            pltpu.VMEM((2, 2, 256, 128), F32),
+            pltpu.VMEM((2, 256, 128), BF16),
+            pltpu.VMEM((2, 256, 128), BF16),
             pltpu.VMEM((4, 128, 512), BF16),
             pltpu.VMEM((2, 8, 128, 256), F32),
             pltpu.VMEM((2, 8, 8, 32, 128), BF16),
             pltpu.VMEM((2, 8, 8, 32, 128), BF16),
             pltpu.VMEM((2, 8, 32, 128), BF16),
             pltpu.VMEM((2, 8, 32, 128), BF16),
-            pltpu.VMEM((16, 16, 256), F32),
-            pltpu.VMEM((16, 16, 256), F32),
-            pltpu.VMEM((16, 16, 256), F32),
+            pltpu.VMEM((128, 256), BF16),
+            pltpu.VMEM((1, 256), F32),
+            pltpu.VMEM((512, 256), BF16),
+            pltpu.VMEM((512, 256), BF16),
+            pltpu.VMEM((2, 32, 128), BF16),
+            pltpu.VMEM((1, 256), F32),
             pltpu.VMEM((16, 8, 256), F32),
+            pltpu.VMEM((16, 8, 256), F32),
+            pltpu.VMEM((16, 8, 256), F32),
+            pltpu.VMEM((16, 8, 256), F32),
+            pltpu.VMEM((8, 256), F32),
+            pltpu.VMEM((16, 8, 256), F32),
+            pltpu.VMEM((16, 8, 256), F32),
+            pltpu.VMEM((8, 256), F32),
         ]
         + [pltpu.SemaphoreType.DMA(shape) for shape in sems],
         compiler_params=pltpu.CompilerParams(
-            collective_id=1, has_side_effects=True, vmem_limit_bytes=40 * 2**20
+            collective_id=1, has_side_effects=True, vmem_limit_bytes=VMEM_BYTES
         ),
     )(features, adjacency, table, weight, bias, cotangent)
+
+
+def finish_kernel(n, *refs):
+    ins, outs, held, sem = refs[:n], refs[n : 2 * n], refs[2 * n : 3 * n], refs[3 * n]
+    loads = [pltpu.make_async_copy(ins[i], held[i], sem.at[0, i]) for i in range(n)]
+    stores = [pltpu.make_async_copy(held[i], outs[i], sem.at[1, i]) for i in range(n)]
+    for copy in loads:
+        copy.start()
+    for load, store in zip(loads, stores):
+        load.wait()
+        store.start()
+    for copy in stores:
+        copy.wait()
+
+
+def finish(*arrays):
+    n = len(arrays)
+    hbm = pl.BlockSpec(memory_space=pltpu.HBM)
+    return pl.pallas_call(
+        functools.partial(finish_kernel, n),
+        name="finish",
+        out_shape=tuple(jax.ShapeDtypeStruct(a.shape, a.dtype) for a in arrays),
+        in_specs=[hbm] * n,
+        out_specs=(hbm,) * n,
+        scratch_shapes=[pltpu.VMEM(a.shape, a.dtype) for a in arrays]
+        + [pltpu.SemaphoreType.DMA((2, n))],
+        compiler_params=pltpu.CompilerParams(vmem_limit_bytes=VMEM_BYTES),
+    )(*arrays)
 
 
 def shards(features, adjacency, tile_coords, tile_counts, weight, bias, cotangent):
@@ -405,6 +538,9 @@
         cotangent,
         scale,
     )
+    hidden, grad_inputs, grad_weight, grad_bias = finish(
+        hidden, grad_inputs, grad_weight, grad_bias
+    )
     return hidden, grad_inputs[None], grad_weight.reshape(128, 256), grad_bias.reshape(256)
 
 

time: 89.7 us -> 77.6 us (0.87)
  local copies, waits for them, and re-layouts: 10.1 us -> 0.6 us
  Pallas kernels: 77.3 us -> 75.2 us
    unnamed x14 -> x0, local copies, waits for them, and re-layouts: 10 us -> none
    pallas_call x1, Pallas kernels: 77.3 us -> 73.4 us  [layer(): pl.pallas_call(functools.partial(kernel, scale), name='layer', out_shape=...]
    pallas_call x0 -> x1, Pallas kernels: none -> 1.77 us  [finish(): pl.pallas_call(functools.partial(finish_kernel, n), name='finish', out_sh...]
where the time goes in v2:
time: 77.6 us; the launch traced here: 77.5 us
  Pallas kernels  75.2 us (97%)
  other arithmetic  1.01 us (1%)
    pallas_call x1, Pallas kernels, layer(): pl.pallas_call(functools.partial(kernel, scale), name='layer', out_shape=...  73.4 us
    pallas_call x1, Pallas kernels, finish(): pl.pallas_call(functools.partial(finish_kernel, n), name='finish', out_sh...  1.77 us

profile of v2, /device:TPU:4, one launch (start us, length us, event | category | flops | bytes accessed | tf_op | source)
XLA Modules:
  0.0 77.5 jit_solution(9269679148030515384)
XLA Ops:
  0.6 0.1 add_add_fusion
  0.7 0.8 %compare_select_fusion = s32[2,1,40]{2,1,0:T(1,128)S(1)} fusion(s32[2,2,40]{2,1,0:T(2,128)} %bitcast.10, s32[2]{0:T(128)} %bitcast.12), kind=kLoop, calls=%fused_computation.2 | loop fusion | flops 320 | bytes 968 | tf_op jit(solution)/shard_map/jit(_where)/select_n | solution.py:528
  1.5 0.1 select_reduce_fusion
  1.7 0.6 add.44.tab
  2.2 73.4 %layer.1 = (bf16[512,256]{1,0:T(8,128)(2,1)}, bf16[2,32,128]{2,1,0:T(8,128)(2,1)}, f32[16,8,256]{2,1,0:T(8,128)}, f32[1,256]{1,0:T(1,128)}) custom-call(bf16[2048,128]{1,0:T(8,128)(2,1)} %feat_hbm.1, bf16[80,256,256]{2,1,0:T(8,128)(2,1)} %bitcast.8, s32[128]{0:T(128)} %add.44.tab, bf16[128,256]{1,0:T(8,128)(2,1)} %w_hbm.1, f32[1,256]{1,0:T(1,128)} %bitcast.11, ...), custom_call_target="tpu_custom_call" | custom-call | tf_op jit(solution)/shard_map/layer/pallas_call | solution.py:448
  75.7 1.8 %finish.1 = (bf16[512,256]{1,0:T(8,128)(2,1)}, bf16[2,32,128]{2,1,0:T(8,128)(2,1)}, f32[16,8,256]{2,1,0:T(8,128)}, f32[1,256]{1,0:T(1,128)}) custom-call(bf16[512,256]{1,0:T(8,128)(2,1)} %get-tuple-element.12.refs_0_, bf16[2,32,128]{2,1,0:T(8,128)(2,1)} %get-tuple-element.13.refs_1_, f32[16,8,256]{2,1,0:T(8,128)} %get-tuple-element.14.refs_2_, ...), custom_call_target="tpu_custom_call" | custom-call | tf_op jit(solution)/shard_map/finish/pallas_call | solution.py:510
  (2 shorter events, 0.0 us)

commit v3 on v2

--- a/solution.py
+++ b/solution.py
@@ -12,6 +12,8 @@
 F32 = jnp.float32
 BF16 = jnp.bfloat16
 SLOTS = 80
+CHUNKS = (4, 1)
+KEEP = (32, 16)
 VMEM_BYTES = 62 * 2**20
 XY_ORDER = (1, 3, 4, 5, 7, 2, 6)
 
@@ -34,13 +36,14 @@
 
 def kernel(
     scale,
-    feat_hbm, adj_hbm, tab, w_hbm, b_hbm, cot_hbm,
+    feat_hbm, adj_hbm, coord_hbm, count_hbm, w_hbm, b_hbm, cot_hbm,
     hid_hbm, gin_hbm, gw_hbm, gb_hbm,
-    adj, feat, acc, pf, ps, pr, rt, acct, xs, xr, zs, zr,
+    coord, count, place, line, tab, adj, feat, acc, pf, ps, pr, rt, acct, xs0, xs1, xr0, xr1, xa, zs, zr, zf, yf, yr,
     w_ref, b_ref, cot_ref, hid_ref, gin_ref, gb_ref, wa_s, wa, wb, wc, ba_s, ba, bb, bc,
-    adj_sem, in_sem, out_sem, s1, s2, s3, r12, r3, ps_s, ps_r, rt_s, rt_r,
+    adj_sem, in_sem, tab_sem, out_sem, s1, s2, s3, r12, r3, ps_s, ps_r, rt_s, rt_r,
     wa_ss, wa_rs, wb_ss, wb_rs, wc_ss, wc_rs,
     ba_ss, ba_rs, bb_ss, bb_rs, bc_ss, bc_rs, xs_s, xs_r, zs_s, zs_r,
+    zf_s, zf_r, yf_s, yf_r,
 ):
     row = lax.axis_index("rows")
     rep = lax.axis_index("rep")
@@ -89,99 +92,130 @@
 
     sent = []
 
+    barrier = pltpu.get_barrier_semaphore()
+    greet = [a_peer(k) for k in range(1, 16)]
+    greet += [b_peer(k) for k in range(1, 16)]
+    for peer in greet:
+        pl.semaphore_signal(barrier, inc=1, device_id=peer, device_id_type=MESH)
     part = SLOTS // 4
     for i in range(4):
         pltpu.make_async_copy(
             adj_hbm.at[pl.ds(i * part, part)], adj.at[pl.ds(i * part, part)], adj_sem.at[i]
         ).start()
 
-    small = [(w_hbm, w_ref), (b_hbm, b_ref), (cot_hbm, cot_ref)]
+    small = [(coord_hbm, coord), (count_hbm, count), (w_hbm, w_ref), (b_hbm, b_ref), (cot_hbm, cot_ref)]
     for i, (src, dst) in enumerate(small):
         pltpu.make_async_copy(src, dst, in_sem.at[i]).start()
 
-    barrier = pltpu.get_barrier_semaphore()
-    greet = [a_peer(k) for k in range(1, 16)]
-    greet += [b_peer(k) for k in range(1, 16)]
-    greet.append(rep_peer(3))
-    for peer in greet:
-        pl.semaphore_signal(barrier, inc=1, device_id=peer, device_id_type=MESH)
     pl.semaphore_wait(barrier, len(greet))
 
     my_j = yl * 4 + x
     is_root = [row == (rep * 2 + s) * 8 for s in range(2)]
     in_plane = [z == core * 4 + s * 2 for s in range(2)]
 
-    def root_copy(s, k):
+    def span(s, c):
+        size = 256 // CHUNKS[s]
+        return pl.ds(c * size, size)
+
+    def root_copy(s, c, k):
         px, pyl = xy_at(k)
         j = pyl * 4 + px
+        size = 256 // CHUNKS[s]
         return send(
-            feat_hbm.at[pl.ds(pl.multiple_of(j * 256, 256), 256)], feat.at[s, j],
-            s1.at[s, k], r12.at[s], device(px, pyl, z, yh, core),
+            feat_hbm.at[pl.ds(pl.multiple_of(j * 256 + c * size, size), size)], feat.at[s, j, span(s, c)],
+            s1.at[s, c, k], r12.at[s, c], device(px, pyl, z, yh, core),
         )
 
-    def plane_copy(s, k):
-        return send(feat.at[s, my_j], feat.at[s, my_j], s2.at[s, k], r12.at[s], z_peer(k))
-
-    def side_copy(s, k):
-        return send(feat.at[s, my_j], feat.at[s, my_j], s3.at[s, k], r3.at[s, k], xy_peer(k))
+    def plane_copy(s, c, k):
+        mine = feat.at[s, my_j, span(s, c)]
+        return send(mine, mine, s2.at[s, c, k], r12.at[s, c], z_peer(k))
+
+    def side_copy(s, c, k):
+        mine = feat.at[s, my_j, span(s, c)]
+        return send(mine, mine, s3.at[s, c, k], r3.at[s, c, k], xy_peer(k))
 
     def drain_if(cond, copy, s):
         @pl.when(cond)
         def _():
-            for k in range(1, 8):
-                copy(s, k).wait_send()
+            for c in range(CHUNKS[s]):
+                for k in range(1, 8):
+                    copy(s, c, k).wait_send()
 
     for s in range(2):
         @pl.when(is_root[s])
         def _():
-            for k in XY_ORDER:
-                root_copy(s, k).start()
-            pltpu.make_async_copy(
-                feat_hbm.at[pl.ds(pl.multiple_of(my_j * 256, 256), 256)], feat.at[s, my_j], r12.at[s]
-            ).start()
+            for c in range(CHUNKS[s]):
+                size = 256 // CHUNKS[s]
+                for k in XY_ORDER:
+                    root_copy(s, c, k).start()
+                pltpu.make_async_copy(
+                    feat_hbm.at[pl.ds(pl.multiple_of(my_j * 256 + c * size, size), size)],
+                    feat.at[s, my_j, span(s, c)], r12.at[s, c],
+                ).start()
 
         sent.append(functools.partial(drain_if, is_root[s], root_copy, s))
 
     acc[...] = jnp.zeros_like(acc)
     adj[SLOTS] = jnp.zeros((256, 256), BF16)
 
-    for s in range(2):
-        arrived(feat.at[s, my_j], r12.at[s])
-
-        @pl.when(in_plane[s])
-        def _():
-            for k in (4, 3, 5, 2, 6, 1, 7):
-                plane_copy(s, k).start()
-
-        sent.append(functools.partial(drain_if, in_plane[s], plane_copy, s))
-
-        for k in XY_ORDER:
-            side_copy(s, k).start()
-            sent.append(side_copy(s, k).wait_send)
-
     for i, (src, dst) in enumerate(small):
         arrived(dst, in_sem.at[i])
+    place[...] = jnp.full((8, 128), -1, jnp.int32)
+    slot = lax.broadcasted_iota(jnp.int32, (1, 40), 1)
+    for s in range(2):
+        where = coord[s, pl.ds(0, 1)] * 8 + coord[s, pl.ds(1, 1)] + s * 64
+        place[pl.ds(s, 1), pl.ds(0, 40)] = jnp.where(slot < count[:, s : s + 1], where, -1)
+    by_slot = place[...].T
+    spot = lax.broadcasted_iota(jnp.int32, (128, 128), 1)
+    number = lax.broadcasted_iota(jnp.int32, (128, 128), 0) - SLOTS
+    found = jnp.where(by_slot[:, 0:1] == spot, number, 0)
+    found += jnp.where(by_slot[:, 1:2] == spot, number + 40, 0)
+    line[...] = jnp.sum(found, axis=0, keepdims=True) + SLOTS
+    to_scalar = pltpu.make_async_copy(line, tab, tab_sem)
+    to_scalar.start()
+    to_scalar.wait()
+
+    for s in range(2):
+        @pl.when(in_plane[s])
+        def _():
+            for c in range(CHUNKS[s]):
+                arrived(feat.at[s, my_j, span(s, c)], r12.at[s, c])
+                for k in (4, 3, 5, 2, 6, 1, 7):
+                    plane_copy(s, c, k).start()
+
+        sent.append(functools.partial(drain_if, in_plane[s], plane_copy, s))
+
+    for s in range(2):
+        for c in range(CHUNKS[s]):
+            @pl.when(jnp.logical_not(in_plane[s]))
+            def _():
+                arrived(feat.at[s, my_j, span(s, c)], r12.at[s, c])
+
+            for k in XY_ORDER:
+                side_copy(s, c, k).start()
+                sent.append(side_copy(s, c, k).wait_send)
+
     for i in range(4):
         view = adj.at[pl.ds(i * part, part)]
         arrived(view, adj_sem.at[i])
 
-    def forward(i, carry):
-        s = lax.div(i, 8)
-        k = lax.rem(i, 8)
+    def forward(s, k, carry):
         fx = lax.rem(x - lax.rem(k, 4) + 4, 4)
         fyl = lax.rem(yl + lax.div(k, 4), 2)
         j = fyl * 4 + fx
 
         @pl.when(k > 0)
         def _():
-            arrived(feat.at[s, j], r3.at[s, k])
+            for c in range(CHUNKS[s]):
+                arrived(feat.at[s, j, span(s, c)], r3.at[s, c, k])
 
         column = feat[s, j]
         for p in range(8):
-            acc[p] += mm(adj[tab[s * 64 + p * 8 + j]], column)
+            acc[p] += mm(adj[tab[0, s * 64 + p * 8 + j]], column)
         return carry
 
-    lax.fori_loop(0, 16, forward, 0)
+    for s in range(2):
+        lax.fori_loop(0, 8, functools.partial(forward, s), 0)
 
     far_yh, other = lax.rem(yh + 1, 2), lax.rem(core + 1, 2)
 
@@ -345,8 +379,8 @@
 
     def back_terms(s, q, quarter):
         left = rt[quarter]
-        out = mm(left[:, :256], adj[tab[s * 64 + quarter * 16 + q]])
-        return out + mm(left[:, 256:], adj[tab[s * 64 + quarter * 16 + 8 + q]])
+        out = mm(left[:, :256], adj[tab[0, s * 64 + quarter * 16 + q]])
+        return out + mm(left[:, 256:], adj[tab[0, s * 64 + quarter * 16 + 8 + q]])
 
     def back_own(i, carry):
         s, q = lax.div(i, 8), lax.rem(i, 8)
@@ -371,13 +405,24 @@
         acct[s, q] += back_terms(s, q, quarter_of(2))
         return carry
 
+    step_b()
     lax.fori_loop(0, 16, back_far, 0, unroll=4)
-    step_b()
     arrived(rt.at[quarter_of(3)], rt_r.at[3])
+
+    xs, xr = (xs0, xs1), (xr0, xr1)
 
     def xs_copy(s, k):
         px, pyl = xy_at(k)
-        return send(xs.at[s, pyl * 4 + px], xr.at[s, k], xs_s.at[s, k], xs_r.at[s, k], xy_peer(k))
+        return send(xs[s].at[pyl * 4 + px], xr[s].at[k], xs_s.at[s, k], xs_r.at[s, k], xy_peer(k))
+
+    late = pl.ds(KEEP[1], 32 - KEEP[1])
+
+    def zf_copy(k):
+        return send(xa.at[lax.rem(z + k, 8)], zf.at[k], zf_s.at[k], zf_r.at[k], z_peer(k))
+
+    def yf_copy(k):
+        px, pyl = xy_at(k)
+        return send(yf.at[pyl * 4 + px], yr.at[k], yf_s.at[k], yf_r.at[k], xy_peer(k))
 
     for s in range(2):
         for hk in (1, 0):
@@ -390,37 +435,66 @@
                 for zl in range(2):
                     for px in range(4):
                         at = zl * 128 + px * 32
-                        xs[s, half * 4 + px, zz * 2 + zl] = out[at : at + 32]
+                        keep = KEEP[s]
+                        xs[s][half * 4 + px, zz * 2 + zl] = out[at : at + keep]
+                        if s == 1:
+                            xa[zz * 2 + zl, half * 4 + px] = out[at + keep : at + 32]
                 return carry
 
             lax.fori_loop(0, 4, back_rest, 0, unroll=True)
             for k in (1, 3, 2) if hk == 0 else (4, 5, 7, 6):
                 xs_copy(s, k).start()
                 sent.append(xs_copy(s, k).wait_send)
+    for k in (4, 3, 5, 2, 6, 1, 7):
+        zf_copy(k).start()
+        sent.append(zf_copy(k).wait_send)
 
     step_c()
 
     def zs_copy(s, k):
-        return send(zs.at[s, lax.rem(z + k, 8)], zr.at[s, k], zs_s.at[s, k], zs_r.at[s, k], z_peer(k))
-
-    for s in range(2):
+        rows = pl.ds(0, KEEP[s])
+        return send(
+            zs.at[s, lax.rem(z + k, 8), rows], zr.at[s, k, rows], zs_s.at[s, k], zs_r.at[s, k], z_peer(k)
+        )
+
+    def over_xy(s):
+        rows = pl.ds(0, KEEP[s])
         for k in range(1, 8):
-            arrived(xr.at[s, k], xs_r.at[s, k])
+            arrived(xr[s].at[k], xs_r.at[s, k])
         for zz in range(8):
-            total = xs[s, my_j, zz].astype(F32)
+            total = xs[s][my_j, zz].astype(F32)
             for k in range(1, 8):
-                total += xr[s, k, zz].astype(F32)
-            zs[s, zz] = total.astype(BF16)
+                total += xr[s][k, zz].astype(F32)
+            zs[s, zz, rows] = total.astype(BF16)
         for k in (4, 3, 5, 2, 6, 1, 7):
             zs_copy(s, k).start()
             sent.append(zs_copy(s, k).wait_send)
 
+    over_xy(0)
+    for k in range(1, 8):
+        arrived(zf.at[k], zf_r.at[k])
+    for j in range(8):
+        total = xa[z, j].astype(F32)
+        for k in range(1, 8):
+            total += zf[k, j].astype(F32)
+        yf[j] = total.astype(BF16)
+    for k in XY_ORDER:
+        yf_copy(k).start()
+        sent.append(yf_copy(k).wait_send)
+    over_xy(1)
+
     for s in range(2):
-        total = zs[s, z].astype(F32)
+        rows = pl.ds(0, KEEP[s])
+        total = zs[s, z, rows].astype(F32)
         for k in range(1, 8):
-            arrived(zr.at[s, k], zs_r.at[s, k])
-            total += zr[s, k].astype(F32)
-        gin_ref[s] = total.astype(BF16)
+            arrived(zr.at[s, k, rows], zs_r.at[s, k])
+            total += zr[s, k, rows].astype(F32)
+        gin_ref[s, rows] = total.astype(BF16)
+    total = yf[my_j].astype(F32)
+    for k in range(1, 8):
+        arrived(yr.at[k], yf_r.at[k])
+        total += yr[k].astype(F32)
+    gin_ref[1, late] = total.astype(BF16)
     put(1, gin_ref, gin_hbm)
 
     for k in range(1, 16):
@@ -438,12 +512,12 @@
         drain()
 
 
-def layer(features, adjacency, table, weight, bias, cotangent, scale):
+def layer(features, adjacency, coords, counts, weight, bias, cotangent, scale):
     hbm = pl.BlockSpec(memory_space=pltpu.HBM)
     sems = [
-        (4,), (3,), (4,), (2, 8), (2, 8), (2, 8), (2,), (2, 8), (4,), (4,), (4,), (4,),
+        (4,), (5,), (), (4,), (2, 4, 8), (2, 4, 8), (2, 4, 8), (2, 4), (2, 4, 8), (4,), (4,), (4,), (4,),
         (16,), (16,), (16,), (16,), (16,), (16,), (), (16,), (16,), (16,), (16,), (),
-        (2, 8), (2, 8), (2, 8), (2, 8),
+        (2, 8), (2, 8), (2, 8), (2, 8), (8,), (8,), (8,), (8,),
     ]
     return pl.pallas_call(
         functools.partial(kernel, scale),
@@ -454,9 +528,14 @@
             jax.ShapeDtypeStruct((16, 8, 256), F32),
             jax.ShapeDtypeStruct((1, 256), F32),
         ),
-        in_specs=[hbm, hbm, pl.BlockSpec(memory_space=pltpu.SMEM), hbm, hbm, hbm],
+        in_specs=[hbm] * 7,
         out_specs=(hbm, hbm, hbm, hbm),
         scratch_shapes=[
+            pltpu.VMEM((2, 2, 40), jnp.int32),
+            pltpu.VMEM((1, 2), jnp.int32),
+            pltpu.VMEM((8, 128), jnp.int32),
+            pltpu.VMEM((1, 128), jnp.int32),
+            pltpu.SMEM((1, 128), jnp.int32),
             pltpu.VMEM((SLOTS + 1, 256, 256), BF16),
             pltpu.VMEM((2, 8, 256, 128), BF16),
             pltpu.VMEM((8, 256, 128), F32),
@@ -465,10 +544,16 @@
             pltpu.VMEM((2, 256, 128), BF16),
             pltpu.VMEM((4, 128, 512), BF16),
             pltpu.VMEM((2, 8, 128, 256), F32),
-            pltpu.VMEM((2, 8, 8, 32, 128), BF16),
-            pltpu.VMEM((2, 8, 8, 32, 128), BF16),
+            pltpu.VMEM((8, 8, KEEP[0], 128), BF16),
+            pltpu.VMEM((8, 8, KEEP[1], 128), BF16),
+            pltpu.VMEM((8, 8, KEEP[0], 128), BF16),
+            pltpu.VMEM((8, 8, KEEP[1], 128), BF16),
+            pltpu.VMEM((8, 8, 32 - KEEP[1], 128), BF16),
             pltpu.VMEM((2, 8, 32, 128), BF16),
             pltpu.VMEM((2, 8, 32, 128), BF16),
+            pltpu.VMEM((8, 8, 16, 128), BF16),
+            pltpu.VMEM((8, 16, 128), BF16),
+            pltpu.VMEM((8, 16, 128), BF16),
             pltpu.VMEM((128, 256), BF16),
             pltpu.VMEM((1, 256), F32),
             pltpu.VMEM((512, 256), BF16),
@@ -488,7 +573,7 @@
         compiler_params=pltpu.CompilerParams(
             collective_id=1, has_side_effects=True, vmem_limit_bytes=VMEM_BYTES
         ),
-    )(features, adjacency, table, weight, bias, cotangent)
+    )(features, adjacency, coords, counts, weight, bias, cotangent)
 
 
 def finish_kernel(n, *refs):
@@ -522,17 +607,11 @@
 def shards(features, adjacency, tile_coords, tile_counts, weight, bias, cotangent):
     rows_count = lax.axis_size("rows")
     scale = 1.0 / math.sqrt(features.shape[0] * rows_count)
-    coords = tile_coords[0, 0]
-    counts = tile_counts[0, 0]
-    slot = jnp.arange(40, dtype=jnp.int32)
-    place = jnp.where(slot[None, :] < counts[:, None], coords[:, 0] * 8 + coords[:, 1], -1)
-    hit = place[:, None, :] == jnp.arange(64, dtype=jnp.int32)[None, :, None]
-    number = slot[None, None, :] + 40 * jnp.arange(2, dtype=jnp.int32)[:, None, None] - SLOTS
-    table = SLOTS + jnp.sum(jnp.where(hit, number, 0), axis=2)
     hidden, grad_inputs, grad_weight, grad_bias = layer(
         features,
         adjacency.reshape(SLOTS, 256, 256),
-        table.reshape(128),
+        tile_coords.reshape(2, 2, 40),
+        tile_counts.reshape(1, 2),
         weight,
         bias.reshape(1, 256),
         cotangent,

time: 77.6 us -> 72.8 us (0.938); the launches traced: 77.5 us -> 71.6 us
  Pallas kernels: 75.2 us -> 70.9 us
  other arithmetic: 1.01 us -> 0 us
    pallas_call x1, Pallas kernels: 73.4 us -> 69.1 us  [layer(): pl.pallas_call(functools.partial(kernel, scale), name='layer', out_shape=...]
    select_n x1 -> x0, other arithmetic: 0.83 us -> none  [shards(): jnp.where(slot[None, :] < counts[:, None], coords[:, 0] * 8 + coords[:, 1...]
where the time goes in v3:
time: 72.8 us; the launch traced here: 71.6 us
  Pallas kernels  70.9 us (97%)
    pallas_call x1, Pallas kernels, layer(): pl.pallas_call(functools.partial(kernel, scale), name='layer', out_shape=...  69.1 us
    pallas_call x1, Pallas kernels, finish(): pl.pallas_call(functools.partial(finish_kernel, n), name='finish', out_sh...  1.77 us

profile of v3, /device:TPU:4, one launch (start us, length us, event | category | flops | bytes accessed | tf_op | source)
XLA Modules:
  0.0 71.6 jit_solution(10741566604148007377)
XLA Ops:
  0.6 69.1 %layer.1 = (bf16[512,256]{1,0:T(8,128)(2,1)}, bf16[2,32,128]{2,1,0:T(8,128)(2,1)}, f32[16,8,256]{2,1,0:T(8,128)}, f32[1,256]{1,0:T(1,128)}) custom-call(bf16[2048,128]{1,0:T(8,128)(2,1)} %feat_hbm.1, bf16[80,256,256]{2,1,0:T(8,128)(2,1)} %bitcast.7, s32[2,2,40]{2,1,0:T(2,128)} %bitcast.8, s32[1,2]{1,0:T(1,128)} %bitcast.10, bf16[128,256]{1,0:T(8,128)(2,1)} %w_hbm.1, ...), custom_call_target="tpu_custom_call" | custom-call | tf_op jit(solution)/shard_map/layer/pallas_call | solution.py:522
  69.8 1.8 %finish.1 = (bf16[512,256]{1,0:T(8,128)(2,1)}, bf16[2,32,128]{2,1,0:T(8,128)(2,1)}, f32[16,8,256]{2,1,0:T(8,128)}, f32[1,256]{1,0:T(1,128)}) custom-call(bf16[512,256]{1,0:T(8,128)(2,1)} %get-tuple-element.12.refs_0_, bf16[2,32,128]{2,1,0:T(8,128)(2,1)} %get-tuple-element.13.refs_1_, f32[16,8,256]{2,1,0:T(8,128)} %get-tuple-element.14.refs_2_, ...), custom_call_target="tpu_custom_call" | custom-call | tf_op jit(solution)/shard_map/finish/pallas_call | solution.py:595

commit v4 on v3

--- a/solution.py
+++ b/solution.py
@@ -39,10 +39,10 @@
     feat_hbm, adj_hbm, coord_hbm, count_hbm, w_hbm, b_hbm, cot_hbm,
     hid_hbm, gin_hbm, gw_hbm, gb_hbm,
     coord, count, place, line, tab, adj, feat, acc, pf, ps, pr, rt, acct, xs0, xs1, xr0, xr1, xa, zs, zr, zf, yf, yr,
-    w_ref, b_ref, cot_ref, hid_ref, gin_ref, gb_ref, wa_s, wa, wb, wc, ba_s, ba, bb, bc,
+    w_ref, b_ref, cot_ref, hid_ref, gin_ref, gw_ref, gb_ref, wa_s, wa, wb, wc,
     adj_sem, in_sem, tab_sem, out_sem, s1, s2, s3, r12, r3, ps_s, ps_r, rt_s, rt_r,
     wa_ss, wa_rs, wb_ss, wb_rs, wc_ss, wc_rs,
-    ba_ss, ba_rs, bb_ss, bb_rs, bc_ss, bc_rs, xs_s, xs_r, zs_s, zs_r,
+    xs_s, xs_r, zs_s, zs_r,
     zf_s, zf_r, yf_s, yf_r,
 ):
     row = lax.axis_index("rows")
@@ -215,26 +215,27 @@
         return carry
 
     for s in range(2):
-        lax.fori_loop(0, 8, functools.partial(forward, s), 0)
+        lax.fori_loop(0, 8, functools.partial(forward, s), 0, unroll=2)
 
     far_yh, other = lax.rem(yh + 1, 2), lax.rem(core + 1, 2)
 
     def core_copy(i):
-        quarter = (far_yh, yh)[i] * 2 + other
-        return send(acc.at[pl.ds(quarter * 2, 2)], pf.at[i], ps_s.at[i], ps_r.at[i], rep_peer(1))
+        quarter = (far_yh, yh)[i // 2] * 2 + other
+        return send(acc.at[quarter * 2 + i % 2], pf.at[i // 2, i % 2], ps_s.at[i], ps_r.at[i], rep_peer(1))
 
     def far_copy(h):
-        return send(ps.at[h], pr.at[h], ps_s.at[2 + h], ps_r.at[2 + h], rep_peer(2))
-
-    for i in range(2):
+        return send(ps.at[h], pr.at[h], ps_s.at[4 + h], ps_r.at[4 + h], rep_peer(2))
+
+    for i in range(4):
         core_copy(i).start()
         sent.append(core_copy(i).wait_send)
-    arrived(pf.at[0], ps_r.at[0])
     for h in range(2):
+        arrived(pf.at[0, h], ps_r.at[h])
         ps[h] = (acc[(far_yh * 2 + core) * 2 + h] + pf[0, h]).astype(BF16)
         far_copy(h).start()
         sent.append(far_copy(h).wait_send)
-    arrived(pf.at[1], ps_r.at[1])
+    for h in range(2):
+        arrived(pf.at[1, h], ps_r.at[2 + h])
 
     c0 = math.sqrt(2.0 / math.pi)
     weight = w_ref[...]
@@ -243,7 +244,7 @@
         wsum, bsum = carry
         rows = pl.ds(pl.multiple_of(h * 256, 256), 256)
         total = acc[rep * 2 + h] + pf[1, h]
-        arrived(pr.at[h], ps_r.at[2 + h])
+        arrived(pr.at[h], ps_r.at[4 + h])
         total += pr[h].astype(F32)
         agg = total.astype(BF16)
         v = mm(agg, weight) + b_ref[...]
@@ -283,41 +284,20 @@
     put(0, hid_ref, hid_hbm)
 
     for j in range(16):
-        wa_s[j] = wsum[j * 8 : j * 8 + 8]
-    ba_s[...] = bsum
-    first = a_pos == 0
+        for h in range(2):
+            wa_s[j, pl.ds(h * 8, 8)] = wsum[j * 8 : j * 8 + 8, h * 128 : h * 128 + 128]
+        wa_s[j, pl.ds(16, 8)] = bsum[:, (j % 2) * 128 : (j % 2) * 128 + 128]
 
     def wa_copy(k):
         return send(wa_s.at[a_at(k)], wa.at[a_pos], wa_ss.at[k], wa_rs.at[k], a_peer(k))
-
-    def ba_copy():
-        return send(ba_s, ba.at[a_pos], ba_ss, ba_rs.at[a_pos], device(0, 0, z, 0, core))
 
     for k in range(1, 16):
         wa_copy(k).start()
         sent.append(wa_copy(k).wait_send)
     wa[a_pos] = wa_s[a_pos]
 
-    @pl.when(a_pos > 0)
-    def _():
-        ba_copy().start()
-
-    @pl.when(first)
-    def _():
-        ba[0] = bsum
-
-    def ba_drain():
-        @pl.when(a_pos > 0)
-        def _():
-            ba_copy().wait_send()
-
-    sent.append(ba_drain)
-
     def wb_copy(k):
         return send(wb.at[b_pos], wb.at[b_pos], wb_ss.at[k], wb_rs.at[k], b_peer(k))
-
-    def bb_copy(k):
-        return send(bb.at[b_pos], bb.at[b_pos], bb_ss.at[k], bb_rs.at[k], b_peer(k))
 
     def add_up(ref):
         total = ref[0]
@@ -333,27 +313,8 @@
             wb_copy(k).start()
             sent.append(wb_copy(k).wait_send)
 
-        @pl.when(first)
-        def _():
-            for j in range(1, 16):
-                arrived(ba.at[j], ba_rs.at[j])
-            bb[b_pos] = add_up(ba)
-            for k in range(1, 16):
-                bb_copy(k).start()
-
-        sent.append(functools.partial(drain_first, bb_copy))
-
-    def drain_first(copy):
-        @pl.when(first)
-        def _():
-            for k in range(1, 16):
-                copy(k).wait_send()
-
     def wc_copy(k):
         return send(wc.at[a_pos], wc.at[a_pos], wc_ss.at[k], wc_rs.at[k], a_peer(k))
-
-    def bc_copy(k):
-        return send(bc, bc, bc_ss.at[k], bc_rs, a_peer(k))
 
     def step_c():
         for k in range(1, 16):
@@ -362,17 +323,6 @@
         for k in range(1, 16):
             wc_copy(k).start()
             sent.append(wc_copy(k).wait_send)
-
-        @pl.when(first)
-        def _():
-            for k in range(1, 16):
-                arrived(bb.at[lax.rem(b_pos - k + 16, 16)], bb_rs.at[k])
-            total = jnp.sum(add_up(bb), axis=0, keepdims=True) * scale
-            bc[...] = jnp.broadcast_to(total, (8, 256))
-            for k in range(1, 16):
-                bc_copy(k).start()
-
-        sent.append(functools.partial(drain_first, bc_copy))
 
     def quarter_of(k):
         return lax.rem(yh + k // 2, 2) * 2 + lax.rem(core + k % 2, 2)
@@ -499,13 +449,12 @@
 
     for k in range(1, 16):
         arrived(wc.at[lax.rem(a_pos - k + 16, 16)], wc_rs.at[k])
-    put(2, wc, gw_hbm)
-
-    @pl.when(a_pos > 0)
-    def _():
-        arrived(bc, bc_rs)
-
-    gb_ref[...] = bc[pl.ds(0, 1)]
+    for j in range(16):
+        for h in range(2):
+            gw_ref[j, :, pl.ds(h * 128, 128)] = wc[j, pl.ds(h * 8, 8)]
+    for h in range(2):
+        gb_ref[:, pl.ds(h * 128, 128)] = jnp.sum(wc[h, pl.ds(16, 8)], axis=0, keepdims=True)
+    put(2, gw_ref, gw_hbm)
     put(3, gb_ref, gb_hbm)
 
     for drain in sent:
@@ -515,8 +464,8 @@
 def layer(features, adjacency, coords, counts, weight, bias, cotangent, scale):
     hbm = pl.BlockSpec(memory_space=pltpu.HBM)
     sems = [
-        (4,), (5,), (), (4,), (2, 4, 8), (2, 4, 8), (2, 4, 8), (2, 4), (2, 4, 8), (4,), (4,), (4,), (4,),
-        (16,), (16,), (16,), (16,), (16,), (16,), (), (16,), (16,), (16,), (16,), (),
+        (4,), (5,), (), (4,), (2, 4, 8), (2, 4, 8), (2, 4, 8), (2, 4), (2, 4, 8), (8,), (8,), (4,), (4,),
+        (16,), (16,), (16,), (16,), (16,), (16,),
         (2, 8), (2, 8), (2, 8), (2, 8), (8,), (8,), (8,), (8,),
     ]
     return pl.pallas_call(
@@ -559,15 +508,12 @@
             pltpu.VMEM((512, 256), BF16),
             pltpu.VMEM((512, 256), BF16),
             pltpu.VMEM((2, 32, 128), BF16),
+            pltpu.VMEM((16, 8, 256), F32),
             pltpu.VMEM((1, 256), F32),
-            pltpu.VMEM((16, 8, 256), F32),
-            pltpu.VMEM((16, 8, 256), F32),
-            pltpu.VMEM((16, 8, 256), F32),
-            pltpu.VMEM((16, 8, 256), F32),
-            pltpu.VMEM((8, 256), F32),
-            pltpu.VMEM((16, 8, 256), F32),
-            pltpu.VMEM((16, 8, 256), F32),
-            pltpu.VMEM((8, 256), F32),
+            pltpu.VMEM((16, 24, 128), F32),
+            pltpu.VMEM((16, 24, 128), F32),
+            pltpu.VMEM((16, 24, 128), F32),
+            pltpu.VMEM((16, 24, 128), F32),
         ]
         + [pltpu.SemaphoreType.DMA(shape) for shape in sems],
         compiler_params=pltpu.CompilerParams(

time: 72.8 us -> 71 us (0.975)
  Pallas kernels: 70.9 us -> 69.6 us
    pallas_call x1, Pallas kernels: 69.1 us -> 67.8 us  [layer(): pl.pallas_call(functools.partial(kernel, scale), name='layer', out_shape=...]
where the time goes in v4:
time: 71 us; the launch traced here: 70.2 us
  Pallas kernels  69.6 us (98%)
    pallas_call x1, Pallas kernels, layer(): pl.pallas_call(functools.partial(kernel, scale), name='layer', out_shape=...  67.8 us
    pallas_call x1, Pallas kernels, finish(): pl.pallas_call(functools.partial(finish_kernel, n), name='finish', out_sh...  1.77 us

profile of v4, /device:TPU:4, one launch (start us, length us, event | category | flops | bytes accessed | tf_op | source)
XLA Modules:
  0.0 70.2 jit_solution(16079798175648854028)
XLA Ops:
  0.6 67.8 %layer.1 = (bf16[512,256]{1,0:T(8,128)(2,1)}, bf16[2,32,128]{2,1,0:T(8,128)(2,1)}, f32[16,8,256]{2,1,0:T(8,128)}, f32[1,256]{1,0:T(1,128)}) custom-call(bf16[2048,128]{1,0:T(8,128)(2,1)} %feat_hbm.1, bf16[80,256,256]{2,1,0:T(8,128)(2,1)} %bitcast.7, s32[2,2,40]{2,1,0:T(2,128)} %bitcast.8, s32[1,2]{1,0:T(1,128)} %bitcast.10, bf16[128,256]{1,0:T(8,128)(2,1)} %w_hbm.1, ...), custom_call_target="tpu_custom_call" | custom-call | tf_op jit(solution)/shard_map/layer/pallas_call | solution.py:471
  68.4 1.8 %finish.1 = (bf16[512,256]{1,0:T(8,128)(2,1)}, bf16[2,32,128]{2,1,0:T(8,128)(2,1)}, f32[16,8,256]{2,1,0:T(8,128)}, f32[1,256]{1,0:T(1,128)}) custom-call(bf16[512,256]{1,0:T(8,128)(2,1)} %get-tuple-element.12.refs_0_, bf16[2,32,128]{2,1,0:T(8,128)(2,1)} %get-tuple-element.13.refs_1_, f32[16,8,256]{2,1,0:T(8,128)} %get-tuple-element.14.refs_2_, ...), custom_call_target="tpu_custom_call" | custom-call | tf_op jit(solution)/shard_map/finish/pallas_call | solution.py:541

commit v5 on v4

--- a/solution.py
+++ b/solution.py
@@ -240,6 +240,16 @@
     c0 = math.sqrt(2.0 / math.pi)
     weight = w_ref[...]
 
+    def far_rows(h):
+        return send(rt.at[rep, h], rt.at[rep, h], rt_s.at[h], rt_r.at[h], rep_peer(2))
+
+    def pass_on(h):
+        far = rt.at[lax.rem(yh + 1, 2) * 2 + core, h]
+        return send(far, far, rt_s.at[2 + h], rt_r.at[2 + h], rep_peer(1))
+
+    def near_rows():
+        return send(rt.at[rep], rt.at[rep], rt_s.at[4], rt_r.at[4], rep_peer(1))
+
     def epilogue(h, carry):
         wsum, bsum = carry
         rows = pl.ds(pl.multiple_of(h * 256, 256), 256)
@@ -255,7 +265,9 @@
         slope = half + 0.5 * v * (1.0 - t * t) * (c0 * (1.0 + 0.134145 * v2))
         grad = cot_ref[rows].astype(F32) * slope
         grad_bf = grad.astype(BF16)
-        rt[rep, :, rows] = mm_nt(weight, grad_bf).astype(BF16)
+        rt[rep, h] = mm_nt(weight, grad_bf).astype(BF16)
+        far_rows(h).start()
+        sent.append(far_rows(h).wait_send)
         wsum = wsum + mm_tn(agg, grad_bf)
         bsum = bsum + jnp.sum(grad.reshape(32, 8, 256), axis=0)
         return wsum, bsum
@@ -270,16 +282,8 @@
         copy.start()
         sent.append(copy.wait)
 
-    def rows_copy(k):
-        return send(rt.at[rep], rt.at[rep], rt_s.at[k], rt_r.at[k], rep_peer(k))
-
-    def pass_on():
-        far = rt.at[lax.rem(yh + 1, 2) * 2 + core]
-        return send(far, far, rt_s.at[3], rt_r.at[3], rep_peer(1))
-
-    for k in (2, 1):
-        rows_copy(k).start()
-        sent.append(rows_copy(k).wait_send)
+    near_rows().start()
+    sent.append(near_rows().wait_send)
 
     put(0, hid_ref, hid_hbm)
 
@@ -327,10 +331,11 @@
     def quarter_of(k):
         return lax.rem(yh + k // 2, 2) * 2 + lax.rem(core + k % 2, 2)
 
+    def back_term(s, q, quarter, h):
+        return mm(rt[quarter, h], adj[tab[0, s * 64 + quarter * 16 + h * 8 + q]])
+
     def back_terms(s, q, quarter):
-        left = rt[quarter]
-        out = mm(left[:, :256], adj[tab[0, s * 64 + quarter * 16 + q]])
-        return out + mm(left[:, 256:], adj[tab[0, s * 64 + quarter * 16 + 8 + q]])
+        return back_term(s, q, quarter, 0) + back_term(s, q, quarter, 1)
 
     def back_own(i, carry):
         s, q = lax.div(i, 8), lax.rem(i, 8)
@@ -338,7 +343,7 @@
         return carry
 
     lax.fori_loop(0, 16, back_own, 0, unroll=4)
-    arrived(rt.at[quarter_of(1)], rt_r.at[1])
+    arrived(rt.at[quarter_of(1)], rt_r.at[4])
 
     def back_core(i, carry):
         s, q = lax.div(i, 8), lax.rem(i, 8)
@@ -346,18 +351,20 @@
         return carry
 
     lax.fori_loop(0, 16, back_core, 0, unroll=4)
-    arrived(rt.at[quarter_of(2)], rt_r.at[2])
-    pass_on().start()
-    sent.append(pass_on().wait_send)
-
-    def back_far(i, carry):
+    def back_far(h, i, carry):
         s, q = lax.div(i, 8), lax.rem(i, 8)
-        acct[s, q] += back_terms(s, q, quarter_of(2))
+        acct[s, q] += back_term(s, q, quarter_of(2), h)
         return carry
 
-    step_b()
-    lax.fori_loop(0, 16, back_far, 0, unroll=4)
-    arrived(rt.at[quarter_of(3)], rt_r.at[3])
+    for h in range(2):
+        arrived(rt.at[quarter_of(2), h], rt_r.at[h])
+        pass_on(h).start()
+        sent.append(pass_on(h).wait_send)
+        if h == 1:
+            step_b()
+        lax.fori_loop(0, 16, functools.partial(back_far, h), 0, unroll=4)
+    for h in range(2):
+        arrived(rt.at[quarter_of(3), h], rt_r.at[2 + h])
 
     xs, xr = (xs0, xs1), (xr0, xr1)
 
@@ -464,7 +471,7 @@
 def layer(features, adjacency, coords, counts, weight, bias, cotangent, scale):
     hbm = pl.BlockSpec(memory_space=pltpu.HBM)
     sems = [
-        (4,), (5,), (), (4,), (2, 4, 8), (2, 4, 8), (2, 4, 8), (2, 4), (2, 4, 8), (8,), (8,), (4,), (4,),
+        (4,), (5,), (), (4,), (2, 4, 8), (2, 4, 8), (2, 4, 8), (2, 4), (2, 4, 8), (8,), (8,), (8,), (8,),
         (16,), (16,), (16,), (16,), (16,), (16,),
         (2, 8), (2, 8), (2, 8), (2, 8), (8,), (8,), (8,), (8,),
     ]
@@ -491,7 +498,7 @@
             pltpu.VMEM((2, 2, 256, 128), F32),
             pltpu.VMEM((2, 256, 128), BF16),
             pltpu.VMEM((2, 256, 128), BF16),
-            pltpu.VMEM((4, 128, 512), BF16),
+            pltpu.VMEM((4, 2, 128, 256), BF16),
             pltpu.VMEM((2, 8, 128, 256), F32),
             pltpu.VMEM((8, 8, KEEP[0], 128), BF16),
             pltpu.VMEM((8, 8, KEEP[1], 128), BF16),

time: 71 us -> 70 us (0.986)
  Pallas kernels: 69.6 us -> 68.3 us
    pallas_call x1, Pallas kernels: 67.8 us -> 66.5 us  [layer(): pl.pallas_call(functools.partial(kernel, scale), name='layer', out_shape=...]
where the time goes in v5:
time: 70 us; the launch traced here: 68.9 us
  Pallas kernels  68.3 us (98%)
    pallas_call x1, Pallas kernels, layer(): pl.pallas_call(functools.partial(kernel, scale), name='layer', out_shape=...  66.5 us
    pallas_call x1, Pallas kernels, finish(): pl.pallas_call(functools.partial(finish_kernel, n), name='finish', out_sh...  1.77 us

profile of v5, /device:TPU:4, one launch (start us, length us, event | category | flops | bytes accessed | tf_op | source)
XLA Modules:
  0.0 68.9 jit_solution(14807769266900311922)
XLA Ops:
  0.6 66.5 %layer.1 = (bf16[512,256]{1,0:T(8,128)(2,1)}, bf16[2,32,128]{2,1,0:T(8,128)(2,1)}, f32[16,8,256]{2,1,0:T(8,128)}, f32[1,256]{1,0:T(1,128)}) custom-call(bf16[2048,128]{1,0:T(8,128)(2,1)} %feat_hbm.1, bf16[80,256,256]{2,1,0:T(8,128)(2,1)} %bitcast.7, s32[2,2,40]{2,1,0:T(2,128)} %bitcast.8, s32[1,2]{1,0:T(1,128)} %bitcast.10, bf16[128,256]{1,0:T(8,128)(2,1)} %w_hbm.1, ...), custom_call_target="tpu_custom_call" | custom-call | tf_op jit(solution)/shard_map/layer/pallas_call | solution.py:478
  67.1 1.8 %finish.1 = (bf16[512,256]{1,0:T(8,128)(2,1)}, bf16[2,32,128]{2,1,0:T(8,128)(2,1)}, f32[16,8,256]{2,1,0:T(8,128)}, f32[1,256]{1,0:T(1,128)}) custom-call(bf16[512,256]{1,0:T(8,128)(2,1)} %get-tuple-element.12.refs_0_, bf16[2,32,128]{2,1,0:T(8,128)(2,1)} %get-tuple-element.13.refs_1_, f32[16,8,256]{2,1,0:T(8,128)} %get-tuple-element.14.refs_2_, ...), custom_call_target="tpu_custom_call" | custom-call | tf_op jit(solution)/shard_map/finish/pallas_call | solution.py:548

commit v6 on v5

--- a/solution.py
+++ b/solution.py
@@ -199,7 +199,7 @@
         view = adj.at[pl.ds(i * part, part)]
         arrived(view, adj_sem.at[i])
 
-    def forward(s, k, carry):
+    def landed(s, k):
         fx = lax.rem(x - lax.rem(k, 4) + 4, 4)
         fyl = lax.rem(yl + lax.div(k, 4), 2)
         j = fyl * 4 + fx
@@ -209,13 +209,21 @@
             for c in range(CHUNKS[s]):
                 arrived(feat.at[s, j, span(s, c)], r3.at[s, c, k])
 
-        column = feat[s, j]
+        return j, feat[s, j]
+
+    def forward(s, k, carry):
+        j, column = landed(s, k)
         for p in range(8):
             acc[p] += mm(adj[tab[0, s * 64 + p * 8 + j]], column)
         return carry
 
     for s in range(2):
-        lax.fori_loop(0, 8, functools.partial(forward, s), 0, unroll=2)
+        lax.fori_loop(0, 8 - 2 * s, functools.partial(forward, s), 0, unroll=2)
+    forward(1, 6, 0)
+    last, column = landed(1, 7)
+
+    def last_term(p):
+        acc[p] += mm(adj[tab[0, 64 + p * 8 + last]], column)
 
     far_yh, other = lax.rem(yh + 1, 2), lax.rem(core + 1, 2)
 
@@ -227,8 +235,11 @@
         return send(ps.at[h], pr.at[h], ps_s.at[4 + h], ps_r.at[4 + h], rep_peer(2))
 
     for i in range(4):
+        last_term(((far_yh, yh)[i // 2] * 2 + other) * 2 + i % 2)
         core_copy(i).start()
         sent.append(core_copy(i).wait_send)
+    for i in range(4):
+        last_term(((far_yh, yh)[i // 2] * 2 + core) * 2 + i % 2)
     for h in range(2):
         arrived(pf.at[0, h], ps_r.at[h])
         ps[h] = (acc[(far_yh * 2 + core) * 2 + h] + pf[0, h]).astype(BF16)

time: 70 us -> 70.8 us (1.011)
  no operation moved by 1% of the time
where the time goes in v6:
time: 70.8 us; the launch traced here: 69.6 us
  Pallas kernels  69 us (97%)
    pallas_call x1, Pallas kernels, layer(): pl.pallas_call(functools.partial(kernel, scale), name='layer', out_shape=...  67.2 us
    pallas_call x1, Pallas kernels, finish(): pl.pallas_call(functools.partial(finish_kernel, n), name='finish', out_sh...  1.77 us

profile of v6, /device:TPU:4, one launch (start us, length us, event | category | flops | bytes accessed | tf_op | source)
XLA Modules:
  0.0 69.6 jit_solution(9904201741625410098)
XLA Ops:
  0.6 67.2 %layer.1 = (bf16[512,256]{1,0:T(8,128)(2,1)}, bf16[2,32,128]{2,1,0:T(8,128)(2,1)}, f32[16,8,256]{2,1,0:T(8,128)}, f32[1,256]{1,0:T(1,128)}) custom-call(bf16[2048,128]{1,0:T(8,128)(2,1)} %feat_hbm.1, bf16[80,256,256]{2,1,0:T(8,128)(2,1)} %bitcast.7, s32[2,2,40]{2,1,0:T(2,128)} %bitcast.8, s32[1,2]{1,0:T(1,128)} %bitcast.10, bf16[128,256]{1,0:T(8,128)(2,1)} %w_hbm.1, ...), custom_call_target="tpu_custom_call" | custom-call | tf_op jit(solution)/shard_map/layer/pallas_call | solution.py:489
  67.8 1.8 %finish.1 = (bf16[512,256]{1,0:T(8,128)(2,1)}, bf16[2,32,128]{2,1,0:T(8,128)(2,1)}, f32[16,8,256]{2,1,0:T(8,128)}, f32[1,256]{1,0:T(1,128)}) custom-call(bf16[512,256]{1,0:T(8,128)(2,1)} %get-tuple-element.12.refs_0_, bf16[2,32,128]{2,1,0:T(8,128)(2,1)} %get-tuple-element.13.refs_1_, f32[16,8,256]{2,1,0:T(8,128)} %get-tuple-element.14.refs_2_, ...), custom_call_target="tpu_custom_call" | custom-call | tf_op jit(solution)/shard_map/finish/pallas_call | solution.py:559
